TPU v7x, 256 devices: a whole 4x4x8 slice. The times are simulated.
256 devices in a mesh: row: 128 (over z, x, y_lo, core), col: 2 (over y_hi).
Axes of the slice: x: 4, y: 4 (y_hi: 2, y_lo: 2; y = y_hi * 2 + y_lo), z: 8, core: 2. Of those that a mesh axis runs over, the one named last changes fastest.
Arguments:
- features: bfloat16 [65536, 128], P(('col', 'row')), may hold values from -6 to 6
- tile_values: bfloat16 [128, 2, 256, 128, 128], P('row', 'col'), may hold values from 0 to 3, as said below
- tile_rows: int32 [128, 2, 256], P('row', 'col'), may hold values from 0 to 3, as said below
- tile_cols: int32 [128, 2, 256], P('row', 'col'), may hold values from 0 to 1
- tile_counts: int32 [128, 2, 128], P('row', 'col'), may hold values from 0 to 2, as said below
- labels: int32 [65536], P(('col', 'row')), may hold values from 0 to 171
- w_self: bfloat16 [128, 256], replicated, may hold values from -0.5 to 0.5
- w_neigh: bfloat16 [128, 256], replicated, may hold values from -1 to 1
- bias: bfloat16 [256], replicated, may hold values from -3 to 3
- w_class: bfloat16 [256, 172], replicated, may hold values from -1 to 1
Outputs:
- hidden: bfloat16 [65536, 256], P(('col', 'row'))
- loss: float32 [], replicated
- grad_self: float32 [128, 256], replicated
- grad_neigh: float32 [128, 256], replicated
- grad_bias: float32 [256], replicated
- grad_class: float32 [256, 172], replicated
Inputs may be any that keep to these rules, and one draw needn't show every extreme that they name: `tile_rows`: every slot index is below 4 for rows. `tile_counts`: at most 2 live slots for one source block, reached in every draw; slots at and beyond the count are ignored. `tile_values`: nonnegative edge weights, mostly zero.
All inputs are finite; a program needn't handle non-finite values.
Results may differ from a plain program's by a relative error of at most 0.012.
The roundings to bfloat16 on the way count: a program that leaves them out, or rounds other values in their place, can miss the bound.
Values may be sent and summed in bfloat16 or wider, within the bound.
No kernel may reach another device: no remote copies, remote signals or barrier semaphores. Data moves between devices by JAX's collectives and lax.ppermute only.
A program may use at most 128 MiB of HBM per device.

v0:
```python
import functools

import jax
import jax.numpy as jnp
from jax import lax
from jax.experimental import pallas as pl
from jax.experimental.pallas import tpu as pltpu
from jax.sharding import Mesh, PartitionSpec as P

NZ, NX, NY, NC = 8, 4, 2, 2
ROW = ("z", "x", "yl", "co")
ALL = ("z", "x", "yl", "co", "yh")
SWAP = [(0, 1), (1, 0)]
TILE = 128
F = 128
HID = 256
CLS = 172
BLOCK = 256
NODES = 65536
DEAD = 8
EXTRA = 176
LIMIT = 6 * 2**20
WIDE = 46 * 2**20
VMEM = pl.BlockSpec(memory_space=pltpu.VMEM)
ANY = pl.BlockSpec(memory_space=pl.ANY)
SMEM = pl.BlockSpec(memory_space=pltpu.SMEM)


def index_of(z, x, yl, co):
    return ((z % NZ * NX + x % NX) * NY + yl % NY) * NC + co % NC


def move(value, target, cores=(0, 1)):
    pairs = []
    for z in range(NZ):
        for x in range(NX):
            for yl in range(NY):
                for co in cores:
                    pairs.append((index_of(z, x, yl, co), index_of(*target(z, x, yl, co))))
    return lax.ppermute(value, ROW, pairs)


def first(step):
    return lambda z, x, yl, co: (z, x + step, yl, co) if co == 0 else (z + step, x, yl, co)


def second(step):
    return lambda z, x, yl, co: (z + step, x, yl, co) if co == 0 else (z, x + step, yl, co)


def sources(z, x, yl, core):
    x_steps, z_near, z_far = (0, 1, 3, 2), (0, 1, 7, 2), (6, 3, 5, 4)
    lists = []
    for piece in range(8):
        places = []
        for i in range(4):
            zo0, xo0 = (0, 1, 7, 2, 6, 3, 5, 4)[piece], x_steps[i]
            zo1, xo1 = (z_near if piece < 4 else z_far)[i], (0, 1, 3, 2, 0, 1, 3, 2)[piece]
            zo = jnp.where(core == 0, zo0, zo1)
            xo = jnp.where(core == 0, xo0, xo1)
            for j in range(2):
                places.append(((z - zo) % NZ * NX + (x - xo) % NX) * NY + (yl + j) % NY)
        lists.extend(places)
    return jnp.stack(lists).astype(jnp.int32)


def degree_body(code_ref, tiles_ref, out_ref, held, acc, sems):
    chunk = tiles_ref.shape[0] // sems.shape[0]

    def copy(step):
        part = pl.ds(step * chunk, chunk)
        return pltpu.make_async_copy(tiles_ref.at[part], held.at[part], sems.at[step])

    for step in range(sems.shape[0]):
        copy(step).start()
    acc[...] = jnp.zeros_like(acc)

    @pl.loop(0, sems.shape[0])
    def _(step):
        copy(step).wait()
        for i in range(chunk):
            n = step * chunk + i
            start = pl.multiple_of((code_ref[n] // 2) * TILE, TILE)
            acc[pl.ds(start, TILE), :] += held[n].astype(jnp.float32)

    out_ref[...] = jnp.broadcast_to(
        jnp.sum(acc[: out_ref.shape[0], :], axis=1, keepdims=True), out_ref.shape
    )


def degrees(codes, tiles):
    total = tiles.shape[0]
    return pl.pallas_call(
        degree_body,
        in_specs=[SMEM, ANY],
        out_specs=VMEM,
        out_shape=jax.ShapeDtypeStruct((4 * TILE, TILE), jnp.float32),
        scratch_shapes=[
            pltpu.VMEM(tiles.shape, tiles.dtype),
            pltpu.VMEM((9 * TILE, TILE), jnp.float32),
            pltpu.SemaphoreType.DMA((8,)),
        ],
        compiler_params=pltpu.CompilerParams(vmem_limit_bytes=WIDE),
        cost_estimate=pl.CostEstimate(
            flops=2 * total * TILE**2, bytes_accessed=total * TILE * TILE * 2, transcendentals=0
        ),
    )(codes, tiles)


def hold_body(core_ref, own_ref, mate_ref, out_ref, sems):
    core = core_ref[0]
    one = pltpu.make_async_copy(own_ref.at[:, core], out_ref.at[0], sems.at[0])
    two = pltpu.make_async_copy(mate_ref.at[:, core], out_ref.at[1], sems.at[1])
    one.start()
    two.start()
    one.wait()
    two.wait()


def hold(core, own_tiles, mate_tiles):
    chips = NZ * NX * NY
    shape = (chips, NC, 2, TILE, TILE)
    return pl.pallas_call(
        hold_body,
        in_specs=[SMEM, ANY, ANY],
        out_specs=VMEM,
        out_shape=pltpu.VMEM((2, chips, 2, TILE, TILE), jnp.bfloat16),
        scratch_shapes=[pltpu.SemaphoreType.DMA((2,))],
        compiler_params=pltpu.CompilerParams(vmem_limit_bytes=WIDE),
        cost_estimate=pl.CostEstimate(flops=0, bytes_accessed=2**24, transcendentals=0),
    )(core, own_tiles.reshape(shape), mate_tiles.reshape(shape))


def piece_body(ranges, has_acc, split, through, *refs):
    core_ref, own_code, mate_code, places = refs[:4]
    blocks = refs[4 : 4 + len(ranges)]
    tiles = refs[4 + len(ranges)]
    rest = refs[5 + len(ranges) :]
    acc = rest[-1]
    core = core_ref[0]
    if has_acc:
        acc[: 8 * TILE, :] = rest[0][...]
        outs = rest[1 + through : -1]
    else:
        acc[...] = jnp.zeros_like(acc)
        outs = rest[through:-1]
    for block, (low, high) in zip(blocks, ranges):
        for i in range(high - low):
            place = places[low + i]
            for k in range(4):
                code = (own_code if k < 2 else mate_code)[(place * 2 + core) * 2 + k % 2]
                tile = tiles[k // 2, place, k % 2]
                source = pl.multiple_of(i * BLOCK + (code % 2) * TILE, TILE)
                target = pl.multiple_of((code // 2) * TILE, TILE)
                acc[pl.ds(target, TILE), :] += jnp.dot(
                    tile, block[pl.ds(source, TILE), :], preferred_element_type=jnp.float32
                )
    if split:
        outs[0][...] = acc[: 2 * TILE, :]
        outs[1][...] = acc[2 * TILE : 4 * TILE, :]
        outs[2][...] = acc[4 * TILE : 8 * TILE, :]
    else:
        outs[0][...] = acc[: 8 * TILE, :]


def absorb(tables, ranges, blocks, tiles, acc, split=False, through=()):
    n = sum(high - low for low, high in ranges)
    args = [*tables, *blocks, tiles]
    specs = [SMEM] * 4 + [VMEM] * (len(blocks) + 1)
    if acc is not None:
        args.append(acc)
        specs.append(VMEM)
    rows = (2, 2, 4) if split else (8,)
    shapes = [jax.ShapeDtypeStruct((r * TILE, TILE), jnp.float32) for r in rows]
    outs = [VMEM] * len(rows)
    alias = {}
    for array in through:
        alias[len(args)] = len(outs)
        args.append(array)
        specs.append(ANY)
        shapes.append(jax.ShapeDtypeStruct(array.shape, array.dtype))
        outs.append(ANY)
    out = pl.pallas_call(
        functools.partial(piece_body, ranges, acc is not None, split, len(alias)),
        in_specs=specs,
        out_specs=outs,
        out_shape=shapes,
        input_output_aliases=alias,
        scratch_shapes=[pltpu.VMEM((9 * TILE, TILE), jnp.float32)],
        compiler_params=pltpu.CompilerParams(vmem_limit_bytes=LIMIT),
        cost_estimate=pl.CostEstimate(
            flops=8 * n * TILE**3, bytes_accessed=4 * n * TILE * TILE * 2 + 2**20, transcendentals=0
        ),
    )(*args)
    return out if len(outs) > 1 else out[0]


def assemble_body(count, *refs):
    out = refs[-1 - count]
    low = 0
    for ref in refs[: -1 - 2 * count]:
        out[low : low + ref.shape[0], :] = ref[...]
        low += ref.shape[0]


def assemble(parts, through):
    shape = (sum(p.shape[0] for p in parts), parts[0].shape[1])
    n = len(through)
    return pl.pallas_call(
        functools.partial(assemble_body, n),
        in_specs=[VMEM] * len(parts) + [ANY] * n,
        out_specs=[VMEM] + [ANY] * n,
        out_shape=[jax.ShapeDtypeStruct(shape, parts[0].dtype)]
        + [jax.ShapeDtypeStruct(t.shape, t.dtype) for t in through],
        input_output_aliases={len(parts) + i: 1 + i for i in range(n)},
        compiler_params=pltpu.CompilerParams(vmem_limit_bytes=LIMIT),
        cost_estimate=pl.CostEstimate(flops=0, bytes_accessed=2**20, transcendentals=0),
    )(*parts, *through)


def choose_body(core_ref, fore, back, *refs):
    out_fore, out_back = refs[-2:]

    @pl.when(core_ref[0] == 0)
    def _():
        out_fore[...] = fore[...]
        out_back[...] = back[...]

    @pl.when(core_ref[0] != 0)
    def _():
        low = 0
        for ref in refs[:-2]:
            out_fore[low : low + ref.shape[0], :] = ref[...]
            out_back[low : low + ref.shape[0], :] = ref[...]
            low += ref.shape[0]


def choose(core, fore, back, parts):
    return pl.pallas_call(
        choose_body,
        in_specs=[SMEM] + [VMEM] * (2 + len(parts)),
        out_specs=[VMEM] * 2,
        out_shape=[jax.ShapeDtypeStruct(fore.shape, fore.dtype)] * 2,
        compiler_params=pltpu.CompilerParams(vmem_limit_bytes=LIMIT),
        cost_estimate=pl.CostEstimate(flops=0, bytes_accessed=2**21, transcendentals=0),
    )(core, fore, back, *parts)


def aggregate(own, tiles, own_code, place, swap_core):
    z, x, yl, core, _ = place
    own_code, half_code = own_code
    other = move(own, lambda z, x, yl, co: (z, x, yl + 1, co))
    mate_tiles = move(tiles, swap_core)
    mate_code = move(half_code, swap_core)
    u = jnp.concatenate([own, other])
    a1, b1 = move(u, first(1)), move(u, first(-1))
    a2, b2 = move(u, first(2)), move(u, first(-2))
    degree = degrees(own_code, tiles)
    here, mate_tiles, degree, b2 = assemble([u, a1, b1, a2], [mate_tiles, degree, b2])
    p1, p2 = move(here, second(1)), move(here, second(-1))
    a3, b3 = move(a2, first(1)), move(b2, first(-1))
    core_at = core.reshape(1).astype(jnp.int32)
    tables = (core_at, own_code, mate_code, sources(z, x, yl, core))
    held = hold(core_at, tiles, mate_tiles)
    acc = absorb(tables, [(0, 8)], [here], held, None)
    p1, p2, acc = lax.optimization_barrier((p1, p2, acc))
    p3, p4 = move(p1, second(1)), move(p2, second(-1))
    c4 = move(a2, first(2))
    acc = absorb(tables, [(8, 16), (16, 24)], [p1, p2], held, acc)
    p3, p4, acc = lax.optimization_barrier((p3, p4, acc))
    s3, s4 = choose(core_at, p3, p4, [b2, a3, b3, c4])
    p5, p6 = move(s3, second(1)), move(s4, second(-1))
    other_degree = lax.ppermute(degree[BLOCK:], "yh", SWAP)
    acc = absorb(tables, [(24, 32), (32, 40)], [p3, s4], held, acc)
    p5, p6, acc, other_degree = lax.optimization_barrier((p5, p6, acc, other_degree))
    half = p5.shape[0] // 2
    p7, p8 = move(p5[:half], second(1)), move(p6[half:], second(-1))
    acc = absorb(tables, [(40, 48), (48, 56)], [p5, p6], held, acc)
    p7, p8, acc = lax.optimization_barrier((p7, p8, acc))
    sums = absorb(tables, [(56, 60), (60, 64)], [p7, p8], held, acc, split=True)
    return degree[:BLOCK], other_degree, sums


def put_loss(extra, loss):
    high = loss.astype(jnp.bfloat16).astype(jnp.float32)
    row = lax.broadcasted_iota(jnp.int32, extra.shape, 0)
    return jnp.where(row == 1, high, jnp.where(row == 2, loss - high, extra))


def dense_body(
    feat, mine, mates, theirs, deg_a, deg_b, labels, w_self, w_neigh, bias, w_class, hid_ref, grad_ref
):
    x = feat[...]
    degree = jnp.maximum(deg_a[...] + deg_b[...], 1.0)
    mean = ((mine[...] + mates[:BLOCK, :] + theirs[...]) / degree).astype(jnp.bfloat16)
    pre = (
        jnp.dot(x, w_self[...], preferred_element_type=jnp.float32)
        + jnp.dot(mean, w_neigh[...], preferred_element_type=jnp.float32)
        + bias[...].astype(jnp.float32)
    )
    hidden = jnp.maximum(pre, 0.0).astype(jnp.bfloat16)
    hid_ref[...] = hidden
    logits = lax.dot_general(
        hidden, w_class[...], (((1,), (1,)), ((), ())), preferred_element_type=jnp.float32
    )
    lane = lax.broadcasted_iota(jnp.int32, logits.shape, 1)
    logits = jnp.where(lane < CLS, logits, -1e30)
    shifted = logits - jnp.max(logits, axis=1, keepdims=True)
    logp = shifted - jnp.log(jnp.sum(jnp.exp(shifted), axis=1, keepdims=True))
    hot = lane == labels[...]
    loss = -jnp.sum(jnp.where(hot, logp, 0.0))
    dlogits = ((jnp.exp(logp) - jnp.where(hot, 1.0, 0.0)) * (1.0 / NODES)).astype(jnp.bfloat16)
    rows = (((0,), (0,)), ((), ()))
    dhidden = jnp.dot(dlogits, w_class[...], preferred_element_type=jnp.float32)
    dpre = jnp.where(pre > 0, dhidden, 0.0).astype(jnp.bfloat16)
    grad_ref[:HID, :] = lax.dot_general(
        dlogits, hidden, rows, preferred_element_type=jnp.float32
    ).astype(grad_ref.dtype)
    ones = jnp.ones((16, BLOCK), jnp.bfloat16)
    extra = jnp.dot(ones, dpre, preferred_element_type=jnp.float32)
    grad_ref[EXTRA : EXTRA + 16, :] = put_loss(extra, loss).astype(grad_ref.dtype)
    grad_ref[HID : HID + F, :] = lax.dot_general(
        x, dpre, rows, preferred_element_type=jnp.float32
    ).astype(grad_ref.dtype)
    grad_ref[HID + F :, :] = lax.dot_general(
        mean, dpre, rows, preferred_element_type=jnp.float32
    ).astype(grad_ref.dtype)


def dense(*args):
    return pl.pallas_call(
        dense_body,
        in_specs=[VMEM] * len(args),
        out_specs=[VMEM, VMEM],
        out_shape=[
            jax.ShapeDtypeStruct((BLOCK, HID), jnp.bfloat16),
            jax.ShapeDtypeStruct((HID + 2 * F, HID), jnp.bfloat16),
        ],
        compiler_params=pltpu.CompilerParams(vmem_limit_bytes=LIMIT),
        cost_estimate=pl.CostEstimate(
            flops=2 * BLOCK * HID * 6 * HID, bytes_accessed=2**21, transcendentals=2 * BLOCK * HID
        ),
    )(*args)


def fold_body(count, repeat, place_ref, parts, out_ref):
    share = parts.shape[0] // count
    total = parts[:share, :].astype(jnp.float32)
    for i in range(1, count):
        total += parts[i * share : (i + 1) * share, :].astype(jnp.float32)
    if out_ref.dtype == jnp.bfloat16:
        split = put_loss(total, total[1:2, :] + total[2:3, :])
        total = jnp.where(place_ref[0] == EXTRA // share, split, total)
    for i in range(repeat):
        out_ref[i * share : (i + 1) * share, :] = total.astype(out_ref.dtype)


def fold(place, parts, count, repeat, dtype):
    return pl.pallas_call(
        functools.partial(fold_body, count, repeat),
        in_specs=[SMEM, VMEM],
        out_specs=VMEM,
        out_shape=jax.ShapeDtypeStruct((parts.shape[0] // count * repeat, HID), dtype),
        compiler_params=pltpu.CompilerParams(vmem_limit_bytes=LIMIT),
    )(place, parts)


def finish_body(whole, loss_ref, self_ref, neigh_ref, bias_ref, class_ref):
    def rows(low, count):
        return whole[low : low + count, :].astype(jnp.float32)

    self_ref[...] = rows(HID, F)
    neigh_ref[...] = rows(HID + F, F)
    class_ref[...] = rows(0, EXTRA)[:CLS, :]
    extra = rows(EXTRA, 16)
    bias_ref[...] = extra[:1, :]
    loss_ref[...] = (extra[1:2, :TILE] + extra[2:3, :TILE]) * (1.0 / NODES)


def finish(whole):
    shapes = ((1, TILE), (F, HID), (F, HID), (1, HID), (CLS, HID))
    return pl.pallas_call(
        finish_body,
        in_specs=[VMEM],
        out_specs=[VMEM] * 5,
        out_shape=[jax.ShapeDtypeStruct(s, jnp.float32) for s in shapes],
        compiler_params=pltpu.CompilerParams(vmem_limit_bytes=LIMIT),
    )(whole)


def shards(
    features, tile_values, tile_rows, tile_cols, tile_counts, labels, w_self, w_neigh, bias, w_class
):
    z, x, yl, core, half = (lax.axis_index(a) for a in ALL)
    tiles = tile_values[0, 0]
    rows, cols, counts = tile_rows[0, 0], tile_cols[0, 0], tile_counts[0, 0]
    swap_core = lambda z, x, yl, co: (z, x, yl, co + 1)

    slot = jnp.arange(2, dtype=jnp.int32)[None, :]
    row_at = rows.reshape(-1, 2)
    target = (row_at // 2 != half).astype(jnp.int32) * 2 + row_at % 2
    code = target * 2 + cols.reshape(-1, 2)
    live = slot < counts[:, None]
    own_code = jnp.where(live, code, 2 * DEAD).reshape(-1)
    mate_code = jnp.where(live, code + DEAD, 2 * DEAD).reshape(-1)
    degree, other_degree, (mine, theirs, mates) = aggregate(
        features, tiles, (own_code, mate_code), (z, x, yl, core, half), swap_core
    )
    mates = move(mates, swap_core)
    theirs = lax.ppermute(theirs + mates[BLOCK:], "yh", SWAP)

    hidden, grads = dense(
        features,
        mine,
        mates,
        theirs,
        degree,
        other_degree,
        labels[:, None],
        w_self,
        w_neigh,
        bias[None, :],
        jnp.pad(w_class.T, ((0, HID - CLS), (0, 0))),
    )
    plane = ("x", "yl", "co", "yh")
    members = NX * NY * NC * 2
    member = lax.axis_index(plane).reshape(1).astype(jnp.int32)
    parts = lax.all_to_all(grads, plane, 0, 0, tiled=True)
    parts = lax.all_to_all(fold(member, parts, members, NZ, jnp.float32), "z", 0, 0, tiled=True)
    whole = lax.all_to_all(fold(member, parts, NZ, members, jnp.bfloat16), plane, 0, 0, tiled=True)
    loss, grad_self, grad_neigh, grad_bias, grad_class = finish(whole)
    return hidden, loss[0, 0], grad_self, grad_neigh, grad_bias[0], grad_class.T


def solution(mesh):
    mesh = Mesh(mesh.devices.reshape(NZ, NX, NY, NC, 2), ALL)
    nodes = ("yh",) + ROW
    placed = (
        P(nodes, None),
        P(ROW, "yh", None, None, None),
        P(ROW, "yh", None),
        P(ROW, "yh", None),
        P(ROW, "yh", None),
        P(nodes),
        P(),
        P(),
        P(),
        P(),
    )
    return jax.shard_map(
        shards,
        mesh=mesh,
        in_specs=placed,
        out_specs=(P(nodes, None), P(), P(), P(), P(), P()),
        check_vma=False,
    )
```

profile of v0, /device:TPU:1, one launch (start us, length us, event | category | flops | bytes accessed | tf_op | source)
XLA Modules:
  0.0 120.0 jit_solution(5733597591657068231)
XLA Ops:
  0.6 3.3 %collective-permute-start.5 = (bf16[256,128,128]{2,1,0:T(8,128)(2,1)}, bf16[256,128,128]{2,1,0:T(8,128)(2,1)}, u32[]{:S(2)}, u32[]{:S(2)}) collective-permute-start(bf16[256,128,128]{2,1,0:T(8,128)(2,1)} %bitcast.89), channel_id=1, source_target_pairs={{0,2},{2,0},{4,6},{6,4},{8,10},{10,8},{12,14},{14,12},{16,18},{18,... | collective-permute-start | bytes 25165832 | tf_op jit(solution)/shard_map/ppermute | solution.py:40
  9.2 1.6 %collective-permute-start.2 = (bf16[512,128]{1,0:T(8,128)(2,1)S(1)}, bf16[512,128]{1,0:T(8,128)(2,1)S(1)}, u32[]{:S(2)}, u32[]{:S(2)}) collective-permute-start(bf16[512,128]{1,0:T(8,128)(2,1)S(1)} %constant_dynamic-update-slice_fusion.refs_0_), channel_id=1, source_target_pairs={{0,8},{2,34},{4,12},{6,38},{8,16},{10,42},{12,20},{14,46},{16,24},... | collective-permute-start | bytes 393224 | tf_op jit(solution)/shard_map/ppermute | solution.py:40
  11.9 2.2 %collective-permute-start.6 = (bf16[512,128]{1,0:T(8,128)(2,1)S(1)}, bf16[512,128]{1,0:T(8,128)(2,1)S(1)}, u32[]{:S(2)}, u32[]{:S(2)}) collective-permute-start(bf16[512,128]{1,0:T(8,128)(2,1)S(1)} %constant_dynamic-update-slice_fusion.refs_0_), channel_id=1, source_target_pairs={{0,16},{2,194},{4,20},{6,198},{8,24},{10,202},{12,28},{14,206},{16... | collective-permute-start | bytes 393224 | tf_op jit(solution)/shard_map/ppermute | solution.py:40
  14.1 4.5 %shard_map.145.refs_5_ = f32[512,128]{1,0:T(8,128)S(1)} custom-call(s32[256]{0:T(256)S(1)} %broadcast_select_fusion.code_ref.refs_1_, bf16[256,128,128]{2,1,0:T(8,128)(2,1)} %bitcast.90), custom_call_target="tpu_custom_call" | custom-call | flops 8388608 | bytes 8388608 | tf_op jit(solution)/shard_map/pallas_call | solution.py:93
  22.8 3.0 %collective-permute-start = (s32[256]{0:T(256)S(1)}, s32[256]{0:T(256)S(1)}, u32[]{:S(2)}, u32[]{:S(2)}) collective-permute-start(s32[256]{0:T(256)S(1)} %get-tuple-element.64), channel_id=1, source_target_pairs={{0,2},{2,0},{4,6},{6,4},{8,10},{10,8},{12,14},{14,12},{16,18},{18,... | collective-permute-start | bytes 3080 | tf_op jit(solution)/shard_map/ppermute | solution.py:40
  26.0 3.5 %shard_map.147.refs_5_.refs_6_ = bf16[2,64,2,128,128]{4,3,2,1,0:T(8,128)(2,1)S(1)} custom-call(s32[1]{0:T(128)} %bitcast.core_ref.refs_0_, bf16[64,2,2,128,128]{4,3,2,1,0:T(8,128)(2,1)} %bitcast.91, bf16[64,2,2,128,128]{4,3,2,1,0:T(8,128)(2,1)} %bitcast.70.mate_ref), custom_call_target="tpu_custom_call" | custom-call | bytes 16777216 | tf_op jit(solution)/shard_map/pallas_call | solution.py:123
  30.6 1.7 %collective-permute-start.10 = (bf16[2048,128]{1,0:T(8,128)(2,1)S(1)}, bf16[2048,128]{1,0:T(8,128)(2,1)S(1)}, u32[]{:S(2)}, u32[]{:S(2)}) collective-permute-start(bf16[2048,128]{1,0:T(8,128)(2,1)S(1)} %collective-permute-done.8.refs_5_), channel_id=1, source_target_pairs={{0,224},{2,26},{4,228},{6,30},{8,232},{10,2},{12,236},{14,6},{16,2... | collective-permute-start | bytes 1572872 | tf_op jit(solution)/shard_map/ppermute | solution.py:40
  32.3 3.2 %collective-permute-start.13 = (bf16[512,128]{1,0:T(8,128)(2,1)S(1)}, bf16[512,128]{1,0:T(8,128)(2,1)S(1)}, u32[]{:S(2)}, u32[]{:S(2)}) collective-permute-start(bf16[512,128]{1,0:T(8,128)(2,1)S(1)} %collective-permute-done.4.refs_3_), channel_id=1, source_target_pairs={{0,16},{2,66},{4,20},{6,70},{8,24},{10,74},{12,28},{14,78},{16,0},... | collective-permute-start | bytes 393224 | tf_op jit(solution)/shard_map/ppermute | solution.py:40
  35.5 1.6 %collective-permute-start.12 = (bf16[512,128]{1,0:T(8,128)(2,1)S(1)}, bf16[512,128]{1,0:T(8,128)(2,1)S(1)}, u32[]{:S(2)}, u32[]{:S(2)}) collective-permute-start(bf16[512,128]{1,0:T(8,128)(2,1)S(1)} %get-tuple-element.42.refs_0_), channel_id=1, source_target_pairs={{0,24},{2,226},{4,28},{6,230},{8,0},{10,234},{12,4},{14,238},{16,8... | collective-permute-start | bytes 393224 | tf_op jit(solution)/shard_map/ppermute | solution.py:40
  39.0 5.4 %collective-permute-done.9.fore.refs_4_ = bf16[2048,128]{1,0:T(8,128)(2,1)S(1)} collective-permute-done((bf16[2048,128]{1,0:T(8,128)(2,1)S(1)}, bf16[2048,128]{1,0:T(8,128)(2,1)S(1)}, u32[]{:S(2)}, u32[]{:S(2)}) %collective-permute-start.9) | collective-permute-done | bytes 524320 | tf_op jit(solution)/shard_map/ppermute | solution.py:40
  44.7 2.7 %collective-permute-start.15 = (bf16[2048,128]{1,0:T(8,128)(2,1)S(1)}, bf16[2048,128]{1,0:T(8,128)(2,1)S(1)}, u32[]{:S(2)}, u32[]{:S(2)}) collective-permute-start(bf16[2048,128]{1,0:T(8,128)(2,1)S(1)} %get-tuple-element.44.refs_5_), channel_id=1, source_target_pairs={{0,224},{2,26},{4,228},{6,30},{8,232},{10,2},{12,236},{14,6},{16,2... | collective-permute-start | bytes 1572872 | tf_op jit(solution)/shard_map/ppermute | solution.py:40
  47.4 3.0 %collective-permute-start.16 = (f32[256,128]{1,0:T(8,128)S(1)}, f32[256,128]{1,0:T(8,128)S(1)}, u32[]{:S(2)}, u32[]{:S(2)}) collective-permute-start(f32[256,128]{1,0:T(8,128)S(1)} %get-tuple-element.67), channel_id=1, source_target_pairs={{0,1},{1,0},{2,3},{3,2},{4,5},{5,4},{6,7},{7,6},{8,9},{9,8},{10,11... | collective-permute-start | bytes 393224 | tf_op jit(solution)/shard_map/ppermute | solution.py:273
  50.4 1.5 %shard_map.151.refs_7_ = f32[1024,128]{1,0:T(8,128)S(1)} custom-call(s32[1]{0:T(128)} %bitcast.core_ref.refs_0_, s32[256]{0:T(256)S(1)} %broadcast_select_fusion.code_ref.refs_1_, s32[256]{0:T(256)S(1)} %collective-permute-done.refs_2_, s32[64]{0:T(128)S(1)} %stack.259.refs_3_, bf16[2048,128]{1,0:T(8,128)(2,1)S(1)} %collective-permute-done.9.fore.refs_4_, ...), custom_call_target="tpu_custom_call" | custom-call | flops 268435456 | bytes 3145728 | tf_op jit(solution)/shard_map/pallas_call | solution.py:183
  54.5 2.8 %collective-permute-start.18 = (bf16[1024,128]{1,0:T(8,128)(2,1)S(1)}, bf16[1024,128]{1,0:T(8,128)(2,1)S(1)}, u32[]{:S(2)}, u32[]{:S(2)}) collective-permute-start(bf16[1024,128]{1,0:T(8,128)(2,1)S(1)} %slice.20), channel_id=1, source_target_pairs={{0,224},{2,26},{4,228},{6,30},{8,232},{10,2},{12,236},{14,6},{16,2... | collective-permute-start | bytes 786440 | tf_op jit(solution)/shard_map/ppermute | solution.py:40
  57.2 1.5 %shard_map.152.refs_7_ = f32[1024,128]{1,0:T(8,128)S(1)} custom-call(s32[1]{0:T(128)} %bitcast.core_ref.refs_0_, s32[256]{0:T(256)S(1)} %broadcast_select_fusion.code_ref.refs_1_, s32[256]{0:T(256)S(1)} %collective-permute-done.refs_2_, s32[64]{0:T(128)S(1)} %stack.259.refs_3_, bf16[2048,128]{1,0:T(8,128)(2,1)S(1)} %collective-permute-done.14.refs_4_, ...), custom_call_target="tpu_custom_call" | custom-call | flops 268435456 | bytes 3145728 | tf_op jit(solution)/shard_map/pallas_call | solution.py:183
  58.7 2.1 %collective-permute-done.17.refs_4_ = bf16[1024,128]{1,0:T(8,128)(2,1)S(1)} collective-permute-done((bf16[1024,128]{1,0:T(8,128)(2,1)S(1)}, bf16[1024,128]{1,0:T(8,128)(2,1)S(1)}, u32[]{:S(2)}, u32[]{:S(2)}) %collective-permute-start.17) | collective-permute-done | bytes 262176 | tf_op jit(solution)/shard_map/ppermute | solution.py:40
  61.9 5.3 %collective-permute-start.19 = (f32[512,128]{1,0:T(8,128)S(1)}, f32[512,128]{1,0:T(8,128)S(1)}, u32[]{:S(2)}, u32[]{:S(2)}) collective-permute-start(f32[512,128]{1,0:T(8,128)S(1)} %get-tuple-element.54), channel_id=1, source_target_pairs={{0,2},{2,0},{4,6},{6,4},{8,10},{10,8},{12,14},{14,12},{16,18},{18,... | collective-permute-start | bytes 786440 | tf_op jit(solution)/shard_map/ppermute | solution.py:40
  68.4 3.0 %collective-permute-start.20 = (f32[256,128]{1,0:T(8,128)S(1)}, f32[256,128]{1,0:T(8,128)S(1)}, u32[]{:S(2)}, u32[]{:S(2)}) collective-permute-start(f32[256,128]{1,0:T(8,128)S(1)} %slice_add_fusion), channel_id=1, source_target_pairs={{0,1},{1,0},{2,3},{3,2},{4,5},{5,4},{6,7},{7,6},{8,9},{9,8},{10,11... | collective-permute-start | bytes 393224 | tf_op jit(solution)/shard_map/ppermute | solution.py:410
  71.6 3.1 %collective-permute-done.20.theirs = f32[256,128]{1,0:T(8,128)S(1)} collective-permute-done((f32[256,128]{1,0:T(8,128)S(1)}, f32[256,128]{1,0:T(8,128)S(1)}, u32[]{:S(2)}, u32[]{:S(2)}) %collective-permute-start.20) | collective-permute-done | bytes 131104 | tf_op jit(solution)/shard_map/ppermute | solution.py:410
  74.7 1.6 %shard_map.154 = (bf16[256,256]{1,0:T(8,128)(2,1)}, bf16[512,256]{1,0:T(8,128)(2,1)}) custom-call(bf16[256,128]{1,0:T(8,128)(2,1)S(1)} %copy-done, f32[256,128]{1,0:T(8,128)S(1)} %get-tuple-element.53.mine, f32[512,128]{1,0:T(8,128)S(1)} %collective-permute-done.19.mates, f32[256,128]{1,0:T(8,128)S(1)} %collective-permute-done.20.theirs, ...), custom_call_target="tpu_custom_call" | custom-call | flops 201326592 | bytes 2097152 | tf_op jit(solution)/shard_map/pallas_call | solution.py:331
  76.3 7.0 %all-to-all-start = ((bf16[32,16,256]{2,1,0:T(8,128)(2,1)}), bf16[32,16,256]{2,1,0:T(8,128)(2,1)S(1)}, u32[]{:S(2)}, u32[]{:S(2)}) async-start(bf16[32,16,256]{2,1,0:T(8,128)(2,1)} %bitcast.74), calls=%async_computation | async-start | bytes 524288 | tf_op jit(solution)/shard_map/all_to_all | solution.py:428
  83.3 8.8 %all-to-all-done = bf16[32,16,256]{2,1,0:T(8,128)(2,1)S(1)} async-done(((bf16[32,16,256]{2,1,0:T(8,128)(2,1)}), bf16[32,16,256]{2,1,0:T(8,128)(2,1)S(1)}, u32[]{:S(2)}, u32[]{:S(2)}) %all-to-all-start) | async-done | bytes 262176 | tf_op jit(solution)/shard_map/all_to_all | solution.py:428
  92.2 13.0 %all_to_all.33 = f32[8,16,256]{2,1,0:T(8,128)S(1)} all-to-all(f32[8,16,256]{2,1,0:T(8,128)S(1)} %bitcast.88), channel_id=1, replica_groups=mesh['z'=8,'x'=4,'yl'=2,'co'=2,'yh'=2] {'z'}, dimensions={0} | all-to-all | bytes 262144 | tf_op jit(solution)/shard_map/all_to_all | solution.py:429
  105.3 13.9 %all_to_all.34 = bf16[32,16,256]{2,1,0:T(8,128)(2,1)S(1)} all-to-all(bf16[32,16,256]{2,1,0:T(8,128)(2,1)S(1)} %bitcast.86), channel_id=1, replica_groups=mesh['z'=8,'x'=4,'yl'=2,'co'=2,'yh'=2] {'x','yl','co','yh'}, dimensions={0} | all-to-all | bytes 524288 | tf_op jit(solution)/shard_map/all_to_all | solution.py:430
  (61 shorter events, 19.8 us)
Async XLA Ops:
  0.6 19.4 %collective-permute-start.5 = (bf16[256,128,128]{2,1,0:T(8,128)(2,1)}, bf16[256,128,128]{2,1,0:T(8,128)(2,1)}, u32[]{:S(2)}, u32[]{:S(2)}) collective-permute-start(bf16[256,128,128]{2,1,0:T(8,128)(2,1)} %bitcast.89), channel_id=1, source_target_pairs={{0,2},{2,0},{4,6},{6,4},{8,10},{10,8},{12,14},{14,12},{16,18},{18,... | collective-permute-start | bytes 25165832 | tf_op jit(solution)/shard_map/ppermute | solution.py:40
  4.0 3.9 %collective-permute-start.1 = (bf16[256,128]{1,0:T(8,128)(2,1)}, bf16[256,128]{1,0:T(8,128)(2,1)S(1)}, u32[]{:S(2)}, u32[]{:S(2)}) collective-permute-start(bf16[256,128]{1,0:T(8,128)(2,1)} %feat.1), channel_id=1, source_target_pairs={{0,4},{2,6},{4,0},{6,2},{8,12},{10,14},{12,8},{14,10},{16,20},{18,... | collective-permute-start | bytes 196616 | tf_op jit(solution)/shard_map/ppermute | solution.py:40
  7.8 10.8 %collective-permute-start.4 = (bf16[512,128]{1,0:T(8,128)(2,1)S(1)}, bf16[512,128]{1,0:T(8,128)(2,1)S(1)}, u32[]{:S(2)}, u32[]{:S(2)}) collective-permute-start(bf16[512,128]{1,0:T(8,128)(2,1)S(1)} %constant_dynamic-update-slice_fusion.refs_0_), channel_id=1, source_target_pairs={{0,16},{2,66},{4,20},{6,70},{8,24},{10,74},{12,28},{14,78},{16,0},... | collective-permute-start | bytes 393224 | tf_op jit(solution)/shard_map/ppermute | solution.py:40
  9.2 9.4 %collective-permute-start.2 = (bf16[512,128]{1,0:T(8,128)(2,1)S(1)}, bf16[512,128]{1,0:T(8,128)(2,1)S(1)}, u32[]{:S(2)}, u32[]{:S(2)}) collective-permute-start(bf16[512,128]{1,0:T(8,128)(2,1)S(1)} %constant_dynamic-update-slice_fusion.refs_0_), channel_id=1, source_target_pairs={{0,8},{2,34},{4,12},{6,38},{8,16},{10,42},{12,20},{14,46},{16,24},... | collective-permute-start | bytes 393224 | tf_op jit(solution)/shard_map/ppermute | solution.py:40
  10.8 7.8 %collective-permute-start.3 = (bf16[512,128]{1,0:T(8,128)(2,1)S(1)}, bf16[512,128]{1,0:T(8,128)(2,1)S(1)}, u32[]{:S(2)}, u32[]{:S(2)}) collective-permute-start(bf16[512,128]{1,0:T(8,128)(2,1)S(1)} %constant_dynamic-update-slice_fusion.refs_0_), channel_id=1, source_target_pairs={{0,24},{2,226},{4,28},{6,230},{8,0},{10,234},{12,4},{14,238},{16,8... | collective-permute-start | bytes 393224 | tf_op jit(solution)/shard_map/ppermute | solution.py:40
  11.9 8.1 %collective-permute-start.6 = (bf16[512,128]{1,0:T(8,128)(2,1)S(1)}, bf16[512,128]{1,0:T(8,128)(2,1)S(1)}, u32[]{:S(2)}, u32[]{:S(2)}) collective-permute-start(bf16[512,128]{1,0:T(8,128)(2,1)S(1)} %constant_dynamic-update-slice_fusion.refs_0_), channel_id=1, source_target_pairs={{0,16},{2,194},{4,20},{6,198},{8,24},{10,202},{12,28},{14,206},{16... | collective-permute-start | bytes 393224 | tf_op jit(solution)/shard_map/ppermute | solution.py:40
  20.0 10.6 %collective-permute-start.7 = (bf16[2048,128]{1,0:T(8,128)(2,1)S(1)}, bf16[2048,128]{1,0:T(8,128)(2,1)S(1)}, u32[]{:S(2)}, u32[]{:S(2)}) collective-permute-start(bf16[2048,128]{1,0:T(8,128)(2,1)S(1)} %get-tuple-element.35.refs_4_), channel_id=1, source_target_pairs={{0,32},{2,10},{4,36},{6,14},{8,40},{10,18},{12,44},{14,22},{16,48}... | collective-permute-start | bytes 1572872 | tf_op jit(solution)/shard_map/ppermute | solution.py:40
  21.3 9.3 %collective-permute-start.8 = (bf16[2048,128]{1,0:T(8,128)(2,1)S(1)}, bf16[2048,128]{1,0:T(8,128)(2,1)S(1)}, u32[]{:S(2)}, u32[]{:S(2)}) collective-permute-start(bf16[2048,128]{1,0:T(8,128)(2,1)S(1)} %get-tuple-element.35.refs_4_), channel_id=1, source_target_pairs={{0,224},{2,26},{4,228},{6,30},{8,232},{10,2},{12,236},{14,6},{16,2... | collective-permute-start | bytes 1572872 | tf_op jit(solution)/shard_map/ppermute | solution.py:40
  22.8 6.7 %collective-permute-start = (s32[256]{0:T(256)S(1)}, s32[256]{0:T(256)S(1)}, u32[]{:S(2)}, u32[]{:S(2)}) collective-permute-start(s32[256]{0:T(256)S(1)} %get-tuple-element.64), channel_id=1, source_target_pairs={{0,2},{2,0},{4,6},{6,4},{8,10},{10,8},{12,14},{14,12},{16,18},{18,... | collective-permute-start | bytes 3080 | tf_op jit(solution)/shard_map/ppermute | solution.py:40
  30.6 8.4 %collective-permute-start.10 = (bf16[2048,128]{1,0:T(8,128)(2,1)S(1)}, bf16[2048,128]{1,0:T(8,128)(2,1)S(1)}, u32[]{:S(2)}, u32[]{:S(2)}) collective-permute-start(bf16[2048,128]{1,0:T(8,128)(2,1)S(1)} %collective-permute-done.8.refs_5_), channel_id=1, source_target_pairs={{0,224},{2,26},{4,228},{6,30},{8,232},{10,2},{12,236},{14,6},{16,2... | collective-permute-start | bytes 1572872 | tf_op jit(solution)/shard_map/ppermute | solution.py:40
  32.3 12.1 %collective-permute-start.9 = (bf16[2048,128]{1,0:T(8,128)(2,1)S(1)}, bf16[2048,128]{1,0:T(8,128)(2,1)S(1)}, u32[]{:S(2)}, u32[]{:S(2)}) collective-permute-start(bf16[2048,128]{1,0:T(8,128)(2,1)S(1)} %collective-permute-done.7.refs_4_), channel_id=1, source_target_pairs={{0,32},{2,10},{4,36},{6,14},{8,40},{10,18},{12,44},{14,22},{16,48}... | collective-permute-start | bytes 1572872 | tf_op jit(solution)/shard_map/ppermute | solution.py:40
  32.3 12.1 %collective-permute-start.11 = (bf16[512,128]{1,0:T(8,128)(2,1)S(1)}, bf16[512,128]{1,0:T(8,128)(2,1)S(1)}, u32[]{:S(2)}, u32[]{:S(2)}) collective-permute-start(bf16[512,128]{1,0:T(8,128)(2,1)S(1)} %collective-permute-done.4.refs_3_), channel_id=1, source_target_pairs={{0,8},{2,34},{4,12},{6,38},{8,16},{10,42},{12,20},{14,46},{16,24},... | collective-permute-start | bytes 393224 | tf_op jit(solution)/shard_map/ppermute | solution.py:40
  32.3 12.1 %collective-permute-start.13 = (bf16[512,128]{1,0:T(8,128)(2,1)S(1)}, bf16[512,128]{1,0:T(8,128)(2,1)S(1)}, u32[]{:S(2)}, u32[]{:S(2)}) collective-permute-start(bf16[512,128]{1,0:T(8,128)(2,1)S(1)} %collective-permute-done.4.refs_3_), channel_id=1, source_target_pairs={{0,16},{2,66},{4,20},{6,70},{8,24},{10,74},{12,28},{14,78},{16,0},... | collective-permute-start | bytes 393224 | tf_op jit(solution)/shard_map/ppermute | solution.py:40
  35.5 8.9 %collective-permute-start.12 = (bf16[512,128]{1,0:T(8,128)(2,1)S(1)}, bf16[512,128]{1,0:T(8,128)(2,1)S(1)}, u32[]{:S(2)}, u32[]{:S(2)}) collective-permute-start(bf16[512,128]{1,0:T(8,128)(2,1)S(1)} %get-tuple-element.42.refs_0_), channel_id=1, source_target_pairs={{0,24},{2,226},{4,28},{6,230},{8,0},{10,234},{12,4},{14,238},{16,8... | collective-permute-start | bytes 393224 | tf_op jit(solution)/shard_map/ppermute | solution.py:40
  44.6 9.6 %collective-permute-start.14 = (bf16[2048,128]{1,0:T(8,128)(2,1)S(1)}, bf16[2048,128]{1,0:T(8,128)(2,1)S(1)}, u32[]{:S(2)}, u32[]{:S(2)}) collective-permute-start(bf16[2048,128]{1,0:T(8,128)(2,1)S(1)} %get-tuple-element.43), channel_id=1, source_target_pairs={{0,32},{2,10},{4,36},{6,14},{8,40},{10,18},{12,44},{14,22},{16,48}... | collective-permute-start | bytes 1572872 | tf_op jit(solution)/shard_map/ppermute | solution.py:40
  44.7 9.5 %collective-permute-start.15 = (bf16[2048,128]{1,0:T(8,128)(2,1)S(1)}, bf16[2048,128]{1,0:T(8,128)(2,1)S(1)}, u32[]{:S(2)}, u32[]{:S(2)}) collective-permute-start(bf16[2048,128]{1,0:T(8,128)(2,1)S(1)} %get-tuple-element.44.refs_5_), channel_id=1, source_target_pairs={{0,224},{2,26},{4,228},{6,30},{8,232},{10,2},{12,236},{14,6},{16,2... | collective-permute-start | bytes 1572872 | tf_op jit(solution)/shard_map/ppermute | solution.py:40
  47.4 5.4 %collective-permute-start.16 = (f32[256,128]{1,0:T(8,128)S(1)}, f32[256,128]{1,0:T(8,128)S(1)}, u32[]{:S(2)}, u32[]{:S(2)}) collective-permute-start(f32[256,128]{1,0:T(8,128)S(1)} %get-tuple-element.67), channel_id=1, source_target_pairs={{0,1},{1,0},{2,3},{3,2},{4,5},{5,4},{6,7},{7,6},{8,9},{9,8},{10,11... | collective-permute-start | bytes 393224 | tf_op jit(solution)/shard_map/ppermute | solution.py:273
  54.3 6.5 %collective-permute-start.17 = (bf16[1024,128]{1,0:T(8,128)(2,1)S(1)}, bf16[1024,128]{1,0:T(8,128)(2,1)S(1)}, u32[]{:S(2)}, u32[]{:S(2)}) collective-permute-start(bf16[1024,128]{1,0:T(8,128)(2,1)S(1)} %slice.19), channel_id=1, source_target_pairs={{0,32},{2,10},{4,36},{6,14},{8,40},{10,18},{12,44},{14,22},{16,48}... | collective-permute-start | bytes 786440 | tf_op jit(solution)/shard_map/ppermute | solution.py:40
  54.4 20.2 %copy-start = (bf16[256,128]{1,0:T(8,128)(2,1)S(1)}, bf16[256,128]{1,0:T(8,128)(2,1)}, u32[]{:S(2)}) copy-start(bf16[256,128]{1,0:T(8,128)(2,1)} %feat.1) | copy-start | bytes 196612
  54.4 20.2 %copy-start.1 = (bf16[128,256]{1,0:T(8,128)(2,1)S(1)}, bf16[128,256]{1,0:T(8,128)(2,1)}, u32[]{:S(2)}) copy-start(bf16[128,256]{1,0:T(8,128)(2,1)} %w_self.1) | copy-start | bytes 196612
  54.5 6.3 %collective-permute-start.18 = (bf16[1024,128]{1,0:T(8,128)(2,1)S(1)}, bf16[1024,128]{1,0:T(8,128)(2,1)S(1)}, u32[]{:S(2)}, u32[]{:S(2)}) collective-permute-start(bf16[1024,128]{1,0:T(8,128)(2,1)S(1)} %slice.20), channel_id=1, source_target_pairs={{0,224},{2,26},{4,228},{6,30},{8,232},{10,2},{12,236},{14,6},{16,2... | collective-permute-start | bytes 786440 | tf_op jit(solution)/shard_map/ppermute | solution.py:40
  61.9 6.4 %collective-permute-start.19 = (f32[512,128]{1,0:T(8,128)S(1)}, f32[512,128]{1,0:T(8,128)S(1)}, u32[]{:S(2)}, u32[]{:S(2)}) collective-permute-start(f32[512,128]{1,0:T(8,128)S(1)} %get-tuple-element.54), channel_id=1, source_target_pairs={{0,2},{2,0},{4,6},{6,4},{8,10},{10,8},{12,14},{14,12},{16,18},{18,... | collective-permute-start | bytes 786440 | tf_op jit(solution)/shard_map/ppermute | solution.py:40
  68.4 6.3 %collective-permute-start.20 = (f32[256,128]{1,0:T(8,128)S(1)}, f32[256,128]{1,0:T(8,128)S(1)}, u32[]{:S(2)}, u32[]{:S(2)}) collective-permute-start(f32[256,128]{1,0:T(8,128)S(1)} %slice_add_fusion), channel_id=1, source_target_pairs={{0,1},{1,0},{2,3},{3,2},{4,5},{5,4},{6,7},{7,6},{8,9},{9,8},{10,11... | collective-permute-start | bytes 393224 | tf_op jit(solution)/shard_map/ppermute | solution.py:410
  76.3 15.9 %all-to-all-start = ((bf16[32,16,256]{2,1,0:T(8,128)(2,1)}), bf16[32,16,256]{2,1,0:T(8,128)(2,1)S(1)}, u32[]{:S(2)}, u32[]{:S(2)}) async-start(bf16[32,16,256]{2,1,0:T(8,128)(2,1)} %bitcast.74), calls=%async_computation | async-start | bytes 524288 | tf_op jit(solution)/shard_map/all_to_all | solution.py:428
  (4 other events, 71.4 us)
where the time goes:
time: 120 us
  starting transfers between devices  45.7 us (38%)
  blocking collectives  27 us (22%)
  waiting for transfers between devices  26.3 us (22%)
  Pallas kernels  17.3 us (14%)
  other arithmetic  1.47 us (1%)
  local copies, waits for them, and re-layouts  1.39 us (1%)
    ppermute x19, starting transfers between devices, move(): return lax.ppermute(value, ROW, pairs)  32.7 us
    all_to_all x1, blocking collectives, shards(): lax.all_to_all(fold(member, parts, NZ, members, jnp.bfloat16), plane, 0,...  13.9 us
    ppermute x19, waiting for transfers between devices, move(): return lax.ppermute(value, ROW, pairs)  13.4 us
    all_to_all x1, blocking collectives, shards(): lax.all_to_all(fold(member, parts, members, NZ, jnp.float32), 'z', 0, 0,...  13 us
    all_to_all x1, waiting for transfers between devices, shards(): parts = lax.all_to_all(grads, plane, 0, 0, tiled=True)  8.85 us
    all_to_all x1, starting transfers between devices, shards(): parts = lax.all_to_all(grads, plane, 0, 0, tiled=True)  6.99 us
    pallas_call x5, Pallas kernels, absorb(): pl.pallas_call(functools.partial(piece_body, ranges, acc is not None, spl...  6.65 us
    pallas_call x1, Pallas kernels, degrees(): pl.pallas_call(degree_body, in_specs=[SMEM, ANY], out_specs=VMEM, out_sha...  4.45 us
  transfers between devices with their start and end apart: 22, of which 10 were waited for; matrix products, arithmetic and copies ran while one was open for 2% of the time, Pallas kernels for 11%

commit v1 on v0

--- a/solution.py
+++ b/solution.py
@@ -254,29 +254,30 @@
     mate_code = move(half_code, swap_core)
     u = jnp.concatenate([own, other])
     a1, b1 = move(u, first(1)), move(u, first(-1))
-    a2, b2 = move(u, first(2)), move(u, first(-2))
+    a2 = move(u, first(2))
     degree = degrees(own_code, tiles)
-    here, mate_tiles, degree, b2 = assemble([u, a1, b1, a2], [mate_tiles, degree, b2])
+    here, mate_tiles, degree = assemble([u, a1, b1, a2], [mate_tiles, degree])
     p1, p2 = move(here, second(1)), move(here, second(-1))
-    a3, b3 = move(a2, first(1)), move(b2, first(-1))
+    a3, b2 = move(a2, first(1)), move(b1, first(-1))
     core_at = core.reshape(1).astype(jnp.int32)
     tables = (core_at, own_code, mate_code, sources(z, x, yl, core))
     held = hold(core_at, tiles, mate_tiles)
     acc = absorb(tables, [(0, 8)], [here], held, None)
-    p1, p2, acc = lax.optimization_barrier((p1, p2, acc))
+    p1, p2, a3, b2, acc = lax.optimization_barrier((p1, p2, a3, b2, acc))
     p3, p4 = move(p1, second(1)), move(p2, second(-1))
-    c4 = move(a2, first(2))
-    acc = absorb(tables, [(8, 16), (16, 24)], [p1, p2], held, acc)
-    p3, p4, acc = lax.optimization_barrier((p3, p4, acc))
+    c4, b3 = move(a3, first(1)), move(b2, first(-1))
+    p3, p4, c4, b3, acc = lax.optimization_barrier((p3, p4, c4, b3, acc))
     s3, s4 = choose(core_at, p3, p4, [b2, a3, b3, c4])
+    half = s3.shape[0] // 2
     p5, p6 = move(s3, second(1)), move(s4, second(-1))
+    p7, p8 = move(s3[:half], second(2)), move(s4[half:], second(-2))
+    acc, degree = absorb(
+        tables, [(8, 16), (16, 24), (24, 32), (32, 40)], [p1, p2, p3, s4], held, acc, through=[degree]
+    )
     other_degree = lax.ppermute(degree[BLOCK:], "yh", SWAP)
-    acc = absorb(tables, [(24, 32), (32, 40)], [p3, s4], held, acc)
-    p5, p6, acc, other_degree = lax.optimization_barrier((p5, p6, acc, other_degree))
-    half = p5.shape[0] // 2
-    p7, p8 = move(p5[:half], second(1)), move(p6[half:], second(-1))
+    p5, p6, acc = lax.optimization_barrier((p5, p6, acc))
     acc = absorb(tables, [(40, 48), (48, 56)], [p5, p6], held, acc)
-    p7, p8, acc = lax.optimization_barrier((p7, p8, acc))
+    p7, p8, acc, other_degree = lax.optimization_barrier((p7, p8, acc, other_degree))
     sums = absorb(tables, [(56, 60), (60, 64)], [p7, p8], held, acc, split=True)
     return degree[:BLOCK], other_degree, sums
 
@@ -426,7 +427,7 @@
     members = NX * NY * NC * 2
     member = lax.axis_index(plane).reshape(1).astype(jnp.int32)
     parts = lax.all_to_all(grads, plane, 0, 0, tiled=True)
-    parts = lax.all_to_all(fold(member, parts, members, NZ, jnp.float32), "z", 0, 0, tiled=True)
+    parts = lax.all_to_all(fold(member, parts, members, NZ, jnp.bfloat16), "z", 0, 0, tiled=True)
     whole = lax.all_to_all(fold(member, parts, NZ, members, jnp.bfloat16), plane, 0, 0, tiled=True)
     loss, grad_self, grad_neigh, grad_bias, grad_class = finish(whole)
     return hidden, loss[0, 0], grad_self, grad_neigh, grad_bias[0], grad_class.T

time: 120 us -> 115 us (0.958)
  starting transfers between devices: 45.7 us -> 42.7 us
  blocking collectives: 27 us -> 25.6 us
    ppermute x19, starting transfers between devices: 32.7 us -> 30.9 us  [move(): return lax.ppermute(value, ROW, pairs)]
    pallas_call x5 -> x4, Pallas kernels: 6.65 us -> 5.88 us  [absorb(): pl.pallas_call(functools.partial(piece_body, ranges, acc is not None, spl...]
  transfers between devices with their start and end apart: 22 -> 22, of which waited for: 10 -> 9; matrix products, arithmetic and copies ran while one was open for 2% -> 2% of each run, Pallas kernels for 11% -> 11%
where the time goes in v1:
time: 115 us
  starting transfers between devices  42.7 us (37%)
  waiting for transfers between devices  26 us (23%)
  blocking collectives  25.6 us (22%)
  Pallas kernels  16.5 us (14%)
  other arithmetic  1.47 us (1%)
  local copies, waits for them, and re-layouts  1.38 us (1%)
    ppermute x19, starting transfers between devices, move(): return lax.ppermute(value, ROW, pairs)  30.9 us
    ppermute x19, waiting for transfers between devices, move(): return lax.ppermute(value, ROW, pairs)  14.1 us
    all_to_all x1, blocking collectives, shards(): lax.all_to_all(fold(member, parts, NZ, members, jnp.bfloat16), plane, 0,...  13.7 us
    all_to_all x1, blocking collectives, shards(): lax.all_to_all(fold(member, parts, members, NZ, jnp.bfloat16), 'z', 0, 0,...  12 us
    all_to_all x1, waiting for transfers between devices, shards(): parts = lax.all_to_all(grads, plane, 0, 0, tiled=True)  8.85 us
    pallas_call x4, Pallas kernels, absorb(): pl.pallas_call(functools.partial(piece_body, ranges, acc is not None, spl...  5.88 us
    all_to_all x1, starting transfers between devices, shards(): parts = lax.all_to_all(grads, plane, 0, 0, tiled=True)  5.83 us
    pallas_call x1, Pallas kernels, degrees(): pl.pallas_call(degree_body, in_specs=[SMEM, ANY], out_specs=VMEM, out_sha...  4.46 us
  transfers between devices with their start and end apart: 22, of which 9 were waited for; matrix products, arithmetic and copies ran while one was open for 2% of the time, Pallas kernels for 11%

profile of v1, /device:TPU:1, one launch (start us, length us, event | category | flops | bytes accessed | tf_op | source)
XLA Modules:
  0.0 114.6 jit_solution(16521166845185348353)
XLA Ops:
  0.6 3.3 %collective-permute-start.5 = (bf16[256,128,128]{2,1,0:T(8,128)(2,1)}, bf16[256,128,128]{2,1,0:T(8,128)(2,1)}, u32[]{:S(2)}, u32[]{:S(2)}) collective-permute-start(bf16[256,128,128]{2,1,0:T(8,128)(2,1)} %bitcast.89), channel_id=1, source_target_pairs={{0,2},{2,0},{4,6},{6,4},{8,10},{10,8},{12,14},{14,12},{16,18},{18,... | collective-permute-start | bytes 25165832 | tf_op jit(solution)/shard_map/ppermute | solution.py:40
  7.8 3.9 %collective-permute-start.3 = (bf16[512,128]{1,0:T(8,128)(2,1)S(1)}, bf16[512,128]{1,0:T(8,128)(2,1)S(1)}, u32[]{:S(2)}, u32[]{:S(2)}) collective-permute-start(bf16[512,128]{1,0:T(8,128)(2,1)S(1)} %constant_dynamic-update-slice_fusion.refs_0_), channel_id=1, source_target_pairs={{0,24},{2,226},{4,28},{6,230},{8,0},{10,234},{12,4},{14,238},{16,8... | collective-permute-start | bytes 393224 | tf_op jit(solution)/shard_map/ppermute | solution.py:40
  11.8 4.5 %shard_map.145.refs_5_ = f32[512,128]{1,0:T(8,128)S(1)} custom-call(s32[256]{0:T(256)S(1)} %broadcast_select_fusion.code_ref.refs_1_, bf16[256,128,128]{2,1,0:T(8,128)(2,1)} %bitcast.90), custom_call_target="tpu_custom_call" | custom-call | flops 8388608 | bytes 8388608 | tf_op jit(solution)/shard_map/pallas_call | solution.py:93
  16.2 2.3 %collective-permute-done.4.refs_3_ = bf16[512,128]{1,0:T(8,128)(2,1)S(1)} collective-permute-done((bf16[512,128]{1,0:T(8,128)(2,1)S(1)}, bf16[512,128]{1,0:T(8,128)(2,1)S(1)}, u32[]{:S(2)}, u32[]{:S(2)}) %collective-permute-start.4) | collective-permute-done | bytes 131104 | tf_op jit(solution)/shard_map/ppermute | solution.py:40
  21.5 2.6 %collective-permute-start.9 = (bf16[512,128]{1,0:T(8,128)(2,1)S(1)}, bf16[512,128]{1,0:T(8,128)(2,1)S(1)}, u32[]{:S(2)}, u32[]{:S(2)}) collective-permute-start(bf16[512,128]{1,0:T(8,128)(2,1)S(1)} %collective-permute-done.3.refs_2_), channel_id=1, source_target_pairs={{0,24},{2,226},{4,28},{6,230},{8,0},{10,234},{12,4},{14,238},{16,8... | collective-permute-start | bytes 393224 | tf_op jit(solution)/shard_map/ppermute | solution.py:40
  24.1 2.9 %collective-permute-start = (s32[256]{0:T(256)S(1)}, s32[256]{0:T(256)S(1)}, u32[]{:S(2)}, u32[]{:S(2)}) collective-permute-start(s32[256]{0:T(256)S(1)} %get-tuple-element.74), channel_id=1, source_target_pairs={{0,2},{2,0},{4,6},{6,4},{8,10},{10,8},{12,14},{14,12},{16,18},{18,... | collective-permute-start | bytes 3080 | tf_op jit(solution)/shard_map/ppermute | solution.py:40
  27.1 3.5 %shard_map.147.refs_5_.refs_8_.refs_6_ = bf16[2,64,2,128,128]{4,3,2,1,0:T(8,128)(2,1)S(1)} custom-call(s32[1]{0:T(128)} %bitcast.core_ref.refs_0_, bf16[64,2,2,128,128]{4,3,2,1,0:T(8,128)(2,1)} %bitcast.91, bf16[64,2,2,128,128]{4,3,2,1,0:T(8,128)(2,1)} %bitcast.70.mate_ref), custom_call_target="tpu_custom_call" | custom-call | bytes 16777216 | tf_op jit(solution)/shard_map/pallas_call | solution.py:123
  31.9 2.7 %collective-permute-start.11 = (bf16[2048,128]{1,0:T(8,128)(2,1)S(1)}, bf16[2048,128]{1,0:T(8,128)(2,1)S(1)}, u32[]{:S(2)}, u32[]{:S(2)}) collective-permute-start(bf16[2048,128]{1,0:T(8,128)(2,1)S(1)} %collective-permute-done.7.refs_5_), channel_id=1, source_target_pairs={{0,224},{2,26},{4,228},{6,30},{8,232},{10,2},{12,236},{14,6},{16,2... | collective-permute-start | bytes 1572872 | tf_op jit(solution)/shard_map/ppermute | solution.py:40
  34.6 2.7 %collective-permute-start.13 = (bf16[512,128]{1,0:T(8,128)(2,1)S(1)}, bf16[512,128]{1,0:T(8,128)(2,1)S(1)}, u32[]{:S(2)}, u32[]{:S(2)}) collective-permute-start(bf16[512,128]{1,0:T(8,128)(2,1)S(1)} %collective-permute-done.9.refs_0_), channel_id=1, source_target_pairs={{0,24},{2,226},{4,28},{6,230},{8,0},{10,234},{12,4},{14,238},{16,8... | collective-permute-start | bytes 393224 | tf_op jit(solution)/shard_map/ppermute | solution.py:40
  37.2 4.1 %collective-permute-done.12.refs_3_ = bf16[512,128]{1,0:T(8,128)(2,1)S(1)} collective-permute-done((bf16[512,128]{1,0:T(8,128)(2,1)S(1)}, bf16[512,128]{1,0:T(8,128)(2,1)S(1)}, u32[]{:S(2)}, u32[]{:S(2)}) %collective-permute-start.12) | collective-permute-done | bytes 131104 | tf_op jit(solution)/shard_map/ppermute | solution.py:40
  41.3 1.5 %collective-permute-done.10.fore.refs_6_ = bf16[2048,128]{1,0:T(8,128)(2,1)S(1)} collective-permute-done((bf16[2048,128]{1,0:T(8,128)(2,1)S(1)}, bf16[2048,128]{1,0:T(8,128)(2,1)S(1)}, u32[]{:S(2)}, u32[]{:S(2)}) %collective-permute-start.10) | collective-permute-done | bytes 524320 | tf_op jit(solution)/shard_map/ppermute | solution.py:40
  43.1 2.7 %collective-permute-start.17 = (bf16[2048,128]{1,0:T(8,128)(2,1)S(1)}, bf16[2048,128]{1,0:T(8,128)(2,1)S(1)}, u32[]{:S(2)}, u32[]{:S(2)}) collective-permute-start(bf16[2048,128]{1,0:T(8,128)(2,1)S(1)} %get-tuple-element.52.refs_7_), channel_id=1, source_target_pairs={{0,224},{2,26},{4,228},{6,30},{8,232},{10,2},{12,236},{14,6},{16,2... | collective-permute-start | bytes 1572872 | tf_op jit(solution)/shard_map/ppermute | solution.py:40
  46.8 2.1 %collective-permute-start.15 = (bf16[1024,128]{1,0:T(8,128)(2,1)S(1)}, bf16[1024,128]{1,0:T(8,128)(2,1)S(1)}, u32[]{:S(2)}, u32[]{:S(2)}) collective-permute-start(bf16[1024,128]{1,0:T(8,128)(2,1)S(1)} %slice.19), channel_id=1, source_target_pairs={{0,192},{2,18},{4,196},{6,22},{8,200},{10,26},{12,204},{14,30},{16... | collective-permute-start | bytes 786440 | tf_op jit(solution)/shard_map/ppermute | solution.py:40
  48.8 2.2 %shard_map.150 = (f32[1024,128]{1,0:T(8,128)S(1)}, f32[512,128]{1,0:T(8,128)S(1)}) custom-call(s32[1]{0:T(128)} %bitcast.core_ref.refs_0_, s32[256]{0:T(256)S(1)} %broadcast_select_fusion.code_ref.refs_1_, s32[256]{0:T(256)S(1)} %collective-permute-done.refs_2_, s32[64]{0:T(128)S(1)} %stack.259.refs_3_, ...), custom_call_target="tpu_custom_call", output_to_operand_aliasing={{1}: (10, {})} | custom-call | flops 536870912 | bytes 5242880 | tf_op jit(solution)/shard_map/pallas_call | solution.py:183
  51.0 3.0 %collective-permute-start.18 = (f32[256,128]{1,0:T(8,128)S(1)}, f32[256,128]{1,0:T(8,128)S(1)}, u32[]{:S(2)}, u32[]{:S(2)}) collective-permute-start(f32[256,128]{1,0:T(8,128)S(1)} %get-tuple-element.77), channel_id=1, source_target_pairs={{0,1},{1,0},{2,3},{3,2},{4,5},{5,4},{6,7},{7,6},{8,9},{9,8},{10,11... | collective-permute-start | bytes 393224 | tf_op jit(solution)/shard_map/ppermute | solution.py:277
  54.1 3.4 %collective-permute-done.17.refs_5_ = bf16[2048,128]{1,0:T(8,128)(2,1)S(1)} collective-permute-done((bf16[2048,128]{1,0:T(8,128)(2,1)S(1)}, bf16[2048,128]{1,0:T(8,128)(2,1)S(1)}, u32[]{:S(2)}, u32[]{:S(2)}) %collective-permute-start.17) | collective-permute-done | bytes 524320 | tf_op jit(solution)/shard_map/ppermute | solution.py:40
  60.2 4.0 %collective-permute-start.19 = (f32[512,128]{1,0:T(8,128)S(1)}, f32[512,128]{1,0:T(8,128)S(1)}, u32[]{:S(2)}, u32[]{:S(2)}) collective-permute-start(f32[512,128]{1,0:T(8,128)S(1)} %get-tuple-element.64), channel_id=1, source_target_pairs={{0,2},{2,0},{4,6},{6,4},{8,10},{10,8},{12,14},{14,12},{16,18},{18,... | collective-permute-start | bytes 786440 | tf_op jit(solution)/shard_map/ppermute | solution.py:40
  65.5 3.0 %collective-permute-start.20 = (f32[256,128]{1,0:T(8,128)S(1)}, f32[256,128]{1,0:T(8,128)S(1)}, u32[]{:S(2)}, u32[]{:S(2)}) collective-permute-start(f32[256,128]{1,0:T(8,128)S(1)} %slice_add_fusion), channel_id=1, source_target_pairs={{0,1},{1,0},{2,3},{3,2},{4,5},{5,4},{6,7},{7,6},{8,9},{9,8},{10,11... | collective-permute-start | bytes 393224 | tf_op jit(solution)/shard_map/ppermute | solution.py:411
  68.7 3.1 %collective-permute-done.20.theirs = f32[256,128]{1,0:T(8,128)S(1)} collective-permute-done((f32[256,128]{1,0:T(8,128)S(1)}, f32[256,128]{1,0:T(8,128)S(1)}, u32[]{:S(2)}, u32[]{:S(2)}) %collective-permute-start.20) | collective-permute-done | bytes 131104 | tf_op jit(solution)/shard_map/ppermute | solution.py:411
  71.8 1.6 %shard_map.153 = (bf16[256,256]{1,0:T(8,128)(2,1)}, bf16[512,256]{1,0:T(8,128)(2,1)}) custom-call(bf16[256,128]{1,0:T(8,128)(2,1)S(1)} %copy-done, f32[256,128]{1,0:T(8,128)S(1)} %get-tuple-element.63.mine, f32[512,128]{1,0:T(8,128)S(1)} %collective-permute-done.19.mates, f32[256,128]{1,0:T(8,128)S(1)} %collective-permute-done.20.theirs, ...), custom_call_target="tpu_custom_call" | custom-call | flops 201326592 | bytes 2097152 | tf_op jit(solution)/shard_map/pallas_call | solution.py:332
  73.4 5.8 %all-to-all-start = ((bf16[32,16,256]{2,1,0:T(8,128)(2,1)}), bf16[32,16,256]{2,1,0:T(8,128)(2,1)S(1)}, u32[]{:S(2)}, u32[]{:S(2)}) async-start(bf16[32,16,256]{2,1,0:T(8,128)(2,1)} %bitcast.74), calls=%async_computation | async-start | bytes 524288 | tf_op jit(solution)/shard_map/all_to_all | solution.py:429
  79.3 8.8 %all-to-all-done = bf16[32,16,256]{2,1,0:T(8,128)(2,1)S(1)} async-done(((bf16[32,16,256]{2,1,0:T(8,128)(2,1)}), bf16[32,16,256]{2,1,0:T(8,128)(2,1)S(1)}, u32[]{:S(2)}, u32[]{:S(2)}) %all-to-all-start) | async-done | bytes 262176 | tf_op jit(solution)/shard_map/all_to_all | solution.py:429
  88.2 12.0 %all_to_all.33 = bf16[8,16,256]{2,1,0:T(8,128)(2,1)S(1)} all-to-all(bf16[8,16,256]{2,1,0:T(8,128)(2,1)S(1)} %bitcast.88), channel_id=1, replica_groups=mesh['z'=8,'x'=4,'yl'=2,'co'=2,'yh'=2] {'z'}, dimensions={0} | all-to-all | bytes 131072 | tf_op jit(solution)/shard_map/all_to_all | solution.py:430
  100.2 13.7 %all_to_all.34 = bf16[32,16,256]{2,1,0:T(8,128)(2,1)S(1)} all-to-all(bf16[32,16,256]{2,1,0:T(8,128)(2,1)S(1)} %bitcast.85), channel_id=1, replica_groups=mesh['z'=8,'x'=4,'yl'=2,'co'=2,'yh'=2] {'x','yl','co','yh'}, dimensions={0} | all-to-all | bytes 524288 | tf_op jit(solution)/shard_map/all_to_all | solution.py:431
  (60 shorter events, 14.3 us)
Async XLA Ops:
  0.6 18.0 %collective-permute-start.5 = (bf16[256,128,128]{2,1,0:T(8,128)(2,1)}, bf16[256,128,128]{2,1,0:T(8,128)(2,1)}, u32[]{:S(2)}, u32[]{:S(2)}) collective-permute-start(bf16[256,128,128]{2,1,0:T(8,128)(2,1)} %bitcast.89), channel_id=1, source_target_pairs={{0,2},{2,0},{4,6},{6,4},{8,10},{10,8},{12,14},{14,12},{16,18},{18,... | collective-permute-start | bytes 25165832 | tf_op jit(solution)/shard_map/ppermute | solution.py:40
  4.0 3.9 %collective-permute-start.1 = (bf16[256,128]{1,0:T(8,128)(2,1)}, bf16[256,128]{1,0:T(8,128)(2,1)S(1)}, u32[]{:S(2)}, u32[]{:S(2)}) collective-permute-start(bf16[256,128]{1,0:T(8,128)(2,1)} %feat.1), channel_id=1, source_target_pairs={{0,4},{2,6},{4,0},{6,2},{8,12},{10,14},{12,8},{14,10},{16,20},{18,... | collective-permute-start | bytes 196616 | tf_op jit(solution)/shard_map/ppermute | solution.py:40
  7.8 8.4 %collective-permute-start.3 = (bf16[512,128]{1,0:T(8,128)(2,1)S(1)}, bf16[512,128]{1,0:T(8,128)(2,1)S(1)}, u32[]{:S(2)}, u32[]{:S(2)}) collective-permute-start(bf16[512,128]{1,0:T(8,128)(2,1)S(1)} %constant_dynamic-update-slice_fusion.refs_0_), channel_id=1, source_target_pairs={{0,24},{2,226},{4,28},{6,230},{8,0},{10,234},{12,4},{14,238},{16,8... | collective-permute-start | bytes 393224 | tf_op jit(solution)/shard_map/ppermute | solution.py:40
  11.8 6.8 %collective-permute-start.4 = (bf16[512,128]{1,0:T(8,128)(2,1)S(1)}, bf16[512,128]{1,0:T(8,128)(2,1)S(1)}, u32[]{:S(2)}, u32[]{:S(2)}) collective-permute-start(bf16[512,128]{1,0:T(8,128)(2,1)S(1)} %constant_dynamic-update-slice_fusion.refs_0_), channel_id=1, source_target_pairs={{0,16},{2,66},{4,20},{6,70},{8,24},{10,74},{12,28},{14,78},{16,0},... | collective-permute-start | bytes 393224 | tf_op jit(solution)/shard_map/ppermute | solution.py:40
  11.8 6.8 %collective-permute-start.2 = (bf16[512,128]{1,0:T(8,128)(2,1)S(1)}, bf16[512,128]{1,0:T(8,128)(2,1)S(1)}, u32[]{:S(2)}, u32[]{:S(2)}) collective-permute-start(bf16[512,128]{1,0:T(8,128)(2,1)S(1)} %constant_dynamic-update-slice_fusion.refs_0_), channel_id=1, source_target_pairs={{0,8},{2,34},{4,12},{6,38},{8,16},{10,42},{12,20},{14,46},{16,24},... | collective-permute-start | bytes 393224 | tf_op jit(solution)/shard_map/ppermute | solution.py:40
  18.6 13.1 %collective-permute-start.6 = (bf16[2048,128]{1,0:T(8,128)(2,1)S(1)}, bf16[2048,128]{1,0:T(8,128)(2,1)S(1)}, u32[]{:S(2)}, u32[]{:S(2)}) collective-permute-start(bf16[2048,128]{1,0:T(8,128)(2,1)S(1)} %get-tuple-element.40.refs_4_), channel_id=1, source_target_pairs={{0,32},{2,10},{4,36},{6,14},{8,40},{10,18},{12,44},{14,22},{16,48}... | collective-permute-start | bytes 1572872 | tf_op jit(solution)/shard_map/ppermute | solution.py:40
  19.9 11.9 %collective-permute-start.7 = (bf16[2048,128]{1,0:T(8,128)(2,1)S(1)}, bf16[2048,128]{1,0:T(8,128)(2,1)S(1)}, u32[]{:S(2)}, u32[]{:S(2)}) collective-permute-start(bf16[2048,128]{1,0:T(8,128)(2,1)S(1)} %get-tuple-element.40.refs_4_), channel_id=1, source_target_pairs={{0,224},{2,26},{4,228},{6,30},{8,232},{10,2},{12,236},{14,6},{16,2... | collective-permute-start | bytes 1572872 | tf_op jit(solution)/shard_map/ppermute | solution.py:40
  21.4 10.4 %collective-permute-start.8 = (bf16[512,128]{1,0:T(8,128)(2,1)S(1)}, bf16[512,128]{1,0:T(8,128)(2,1)S(1)}, u32[]{:S(2)}, u32[]{:S(2)}) collective-permute-start(bf16[512,128]{1,0:T(8,128)(2,1)S(1)} %collective-permute-done.4.refs_3_), channel_id=1, source_target_pairs={{0,8},{2,34},{4,12},{6,38},{8,16},{10,42},{12,20},{14,46},{16,24},... | collective-permute-start | bytes 393224 | tf_op jit(solution)/shard_map/ppermute | solution.py:40
  21.5 10.3 %collective-permute-start.9 = (bf16[512,128]{1,0:T(8,128)(2,1)S(1)}, bf16[512,128]{1,0:T(8,128)(2,1)S(1)}, u32[]{:S(2)}, u32[]{:S(2)}) collective-permute-start(bf16[512,128]{1,0:T(8,128)(2,1)S(1)} %collective-permute-done.3.refs_2_), channel_id=1, source_target_pairs={{0,24},{2,226},{4,28},{6,230},{8,0},{10,234},{12,4},{14,238},{16,8... | collective-permute-start | bytes 393224 | tf_op jit(solution)/shard_map/ppermute | solution.py:40
  24.1 6.6 %collective-permute-start = (s32[256]{0:T(256)S(1)}, s32[256]{0:T(256)S(1)}, u32[]{:S(2)}, u32[]{:S(2)}) collective-permute-start(s32[256]{0:T(256)S(1)} %get-tuple-element.74), channel_id=1, source_target_pairs={{0,2},{2,0},{4,6},{6,4},{8,10},{10,8},{12,14},{14,12},{16,18},{18,... | collective-permute-start | bytes 3080 | tf_op jit(solution)/shard_map/ppermute | solution.py:40
  31.8 11.0 %collective-permute-start.10 = (bf16[2048,128]{1,0:T(8,128)(2,1)S(1)}, bf16[2048,128]{1,0:T(8,128)(2,1)S(1)}, u32[]{:S(2)}, u32[]{:S(2)}) collective-permute-start(bf16[2048,128]{1,0:T(8,128)(2,1)S(1)} %collective-permute-done.6.refs_4_), channel_id=1, source_target_pairs={{0,32},{2,10},{4,36},{6,14},{8,40},{10,18},{12,44},{14,22},{16,48}... | collective-permute-start | bytes 1572872 | tf_op jit(solution)/shard_map/ppermute | solution.py:40
  31.9 10.9 %collective-permute-start.11 = (bf16[2048,128]{1,0:T(8,128)(2,1)S(1)}, bf16[2048,128]{1,0:T(8,128)(2,1)S(1)}, u32[]{:S(2)}, u32[]{:S(2)}) collective-permute-start(bf16[2048,128]{1,0:T(8,128)(2,1)S(1)} %collective-permute-done.7.refs_5_), channel_id=1, source_target_pairs={{0,224},{2,26},{4,228},{6,30},{8,232},{10,2},{12,236},{14,6},{16,2... | collective-permute-start | bytes 1572872 | tf_op jit(solution)/shard_map/ppermute | solution.py:40
  34.6 6.8 %collective-permute-start.12 = (bf16[512,128]{1,0:T(8,128)(2,1)S(1)}, bf16[512,128]{1,0:T(8,128)(2,1)S(1)}, u32[]{:S(2)}, u32[]{:S(2)}) collective-permute-start(bf16[512,128]{1,0:T(8,128)(2,1)S(1)} %collective-permute-done.8.refs_1_), channel_id=1, source_target_pairs={{0,8},{2,34},{4,12},{6,38},{8,16},{10,42},{12,20},{14,46},{16,24},... | collective-permute-start | bytes 393224 | tf_op jit(solution)/shard_map/ppermute | solution.py:40
  34.6 6.8 %collective-permute-start.13 = (bf16[512,128]{1,0:T(8,128)(2,1)S(1)}, bf16[512,128]{1,0:T(8,128)(2,1)S(1)}, u32[]{:S(2)}, u32[]{:S(2)}) collective-permute-start(bf16[512,128]{1,0:T(8,128)(2,1)S(1)} %collective-permute-done.9.refs_0_), channel_id=1, source_target_pairs={{0,24},{2,226},{4,28},{6,230},{8,0},{10,234},{12,4},{14,238},{16,8... | collective-permute-start | bytes 393224 | tf_op jit(solution)/shard_map/ppermute | solution.py:40
  43.0 11.1 %collective-permute-start.16 = (bf16[2048,128]{1,0:T(8,128)(2,1)S(1)}, bf16[2048,128]{1,0:T(8,128)(2,1)S(1)}, u32[]{:S(2)}, u32[]{:S(2)}) collective-permute-start(bf16[2048,128]{1,0:T(8,128)(2,1)S(1)} %get-tuple-element.51), channel_id=1, source_target_pairs={{0,32},{2,10},{4,36},{6,14},{8,40},{10,18},{12,44},{14,22},{16,48}... | collective-permute-start | bytes 1572872 | tf_op jit(solution)/shard_map/ppermute | solution.py:40
  43.1 14.4 %collective-permute-start.17 = (bf16[2048,128]{1,0:T(8,128)(2,1)S(1)}, bf16[2048,128]{1,0:T(8,128)(2,1)S(1)}, u32[]{:S(2)}, u32[]{:S(2)}) collective-permute-start(bf16[2048,128]{1,0:T(8,128)(2,1)S(1)} %get-tuple-element.52.refs_7_), channel_id=1, source_target_pairs={{0,224},{2,26},{4,228},{6,30},{8,232},{10,2},{12,236},{14,6},{16,2... | collective-permute-start | bytes 1572872 | tf_op jit(solution)/shard_map/ppermute | solution.py:40
  45.8 13.2 %collective-permute-start.14 = (bf16[1024,128]{1,0:T(8,128)(2,1)S(1)}, bf16[1024,128]{1,0:T(8,128)(2,1)S(1)}, u32[]{:S(2)}, u32[]{:S(2)}) collective-permute-start(bf16[1024,128]{1,0:T(8,128)(2,1)S(1)} %slice.18), channel_id=1, source_target_pairs={{0,64},{2,18},{4,68},{6,22},{8,72},{10,26},{12,76},{14,30},{16,80}... | collective-permute-start | bytes 786440 | tf_op jit(solution)/shard_map/ppermute | solution.py:40
  46.8 12.3 %collective-permute-start.15 = (bf16[1024,128]{1,0:T(8,128)(2,1)S(1)}, bf16[1024,128]{1,0:T(8,128)(2,1)S(1)}, u32[]{:S(2)}, u32[]{:S(2)}) collective-permute-start(bf16[1024,128]{1,0:T(8,128)(2,1)S(1)} %slice.19), channel_id=1, source_target_pairs={{0,192},{2,18},{4,196},{6,22},{8,200},{10,26},{12,204},{14,30},{16... | collective-permute-start | bytes 786440 | tf_op jit(solution)/shard_map/ppermute | solution.py:40
  51.0 7.9 %collective-permute-start.18 = (f32[256,128]{1,0:T(8,128)S(1)}, f32[256,128]{1,0:T(8,128)S(1)}, u32[]{:S(2)}, u32[]{:S(2)}) collective-permute-start(f32[256,128]{1,0:T(8,128)S(1)} %get-tuple-element.77), channel_id=1, source_target_pairs={{0,1},{1,0},{2,3},{3,2},{4,5},{5,4},{6,7},{7,6},{8,9},{9,8},{10,11... | collective-permute-start | bytes 393224 | tf_op jit(solution)/shard_map/ppermute | solution.py:277
  57.5 14.3 %copy-start = (bf16[256,128]{1,0:T(8,128)(2,1)S(1)}, bf16[256,128]{1,0:T(8,128)(2,1)}, u32[]{:S(2)}) copy-start(bf16[256,128]{1,0:T(8,128)(2,1)} %feat.1) | copy-start | bytes 196612
  57.5 14.3 %copy-start.1 = (bf16[128,256]{1,0:T(8,128)(2,1)S(1)}, bf16[128,256]{1,0:T(8,128)(2,1)}, u32[]{:S(2)}) copy-start(bf16[128,256]{1,0:T(8,128)(2,1)} %w_self.1) | copy-start | bytes 196612
  60.2 5.2 %collective-permute-start.19 = (f32[512,128]{1,0:T(8,128)S(1)}, f32[512,128]{1,0:T(8,128)S(1)}, u32[]{:S(2)}, u32[]{:S(2)}) collective-permute-start(f32[512,128]{1,0:T(8,128)S(1)} %get-tuple-element.64), channel_id=1, source_target_pairs={{0,2},{2,0},{4,6},{6,4},{8,10},{10,8},{12,14},{14,12},{16,18},{18,... | collective-permute-start | bytes 786440 | tf_op jit(solution)/shard_map/ppermute | solution.py:40
  65.5 6.3 %collective-permute-start.20 = (f32[256,128]{1,0:T(8,128)S(1)}, f32[256,128]{1,0:T(8,128)S(1)}, u32[]{:S(2)}, u32[]{:S(2)}) collective-permute-start(f32[256,128]{1,0:T(8,128)S(1)} %slice_add_fusion), channel_id=1, source_target_pairs={{0,1},{1,0},{2,3},{3,2},{4,5},{5,4},{6,7},{7,6},{8,9},{9,8},{10,11... | collective-permute-start | bytes 393224 | tf_op jit(solution)/shard_map/ppermute | solution.py:411
  73.4 14.7 %all-to-all-start = ((bf16[32,16,256]{2,1,0:T(8,128)(2,1)}), bf16[32,16,256]{2,1,0:T(8,128)(2,1)S(1)}, u32[]{:S(2)}, u32[]{:S(2)}) async-start(bf16[32,16,256]{2,1,0:T(8,128)(2,1)} %bitcast.74), calls=%async_computation | async-start | bytes 524288 | tf_op jit(solution)/shard_map/all_to_all | solution.py:429
  (4 other events, 47.6 us)

commit v2 on v1

--- a/solution.py
+++ b/solution.py
@@ -277,8 +277,10 @@
     other_degree = lax.ppermute(degree[BLOCK:], "yh", SWAP)
     p5, p6, acc = lax.optimization_barrier((p5, p6, acc))
     acc = absorb(tables, [(40, 48), (48, 56)], [p5, p6], held, acc)
-    p7, p8, acc, other_degree = lax.optimization_barrier((p7, p8, acc, other_degree))
-    sums = absorb(tables, [(56, 60), (60, 64)], [p7, p8], held, acc, split=True)
+    p7, acc, other_degree = lax.optimization_barrier((p7, acc, other_degree))
+    acc = absorb(tables, [(56, 60)], [p7], held, acc)
+    p8, acc = lax.optimization_barrier((p8, acc))
+    sums = absorb(tables, [(60, 64)], [p8], held, acc, split=True)
     return degree[:BLOCK], other_degree, sums
 
 
@@ -293,7 +295,7 @@
 ):
     x = feat[...]
     degree = jnp.maximum(deg_a[...] + deg_b[...], 1.0)
-    mean = ((mine[...] + mates[:BLOCK, :] + theirs[...]) / degree).astype(jnp.bfloat16)
+    mean = ((mine[...] + mates[:BLOCK, :] + theirs[...].astype(jnp.float32)) / degree).astype(jnp.bfloat16)
     pre = (
         jnp.dot(x, w_self[...], preferred_element_type=jnp.float32)
         + jnp.dot(mean, w_neigh[...], preferred_element_type=jnp.float32)
@@ -408,7 +410,7 @@
         features, tiles, (own_code, mate_code), (z, x, yl, core, half), swap_core
     )
     mates = move(mates, swap_core)
-    theirs = lax.ppermute(theirs + mates[BLOCK:], "yh", SWAP)
+    theirs = lax.ppermute((theirs + mates[BLOCK:]).astype(jnp.bfloat16), "yh", SWAP)
 
     hidden, grads = dense(
         features,

time: 115 us -> 114 us (level)
  waiting for transfers between devices: 26 us -> 24.3 us
    ppermute x1, waiting for transfers between devices: 3.1 us -> 1.51 us  [shards(): lax.ppermute((theirs + mates[BLOCK:]).astype(jnp.bfloat16), 'yh', SWAP)]
    pallas_call x4 -> x5, Pallas kernels: 5.88 us -> 6.61 us  [absorb(): pl.pallas_call(functools.partial(piece_body, ranges, acc is not None, spl...]
  transfers between devices with their start and end apart: 22 -> 22, of which waited for: 9 -> 8; matrix products, arithmetic and copies ran while one was open for 2% -> 2% of each run, Pallas kernels for 11% -> 12%
where the time goes in v2:
time: 114 us
  starting transfers between devices  42.3 us (37%)
  blocking collectives  26.3 us (23%)
  waiting for transfers between devices  24.3 us (21%)
  Pallas kernels  17.2 us (15%)
  other arithmetic  1.47 us (1%)
  local copies, waits for them, and re-layouts  1.39 us (1%)
    ppermute x19, starting transfers between devices, move(): return lax.ppermute(value, ROW, pairs)  30 us
    ppermute x19, waiting for transfers between devices, move(): return lax.ppermute(value, ROW, pairs)  14 us
    all_to_all x1, blocking collectives, shards(): lax.all_to_all(fold(member, parts, NZ, members, jnp.bfloat16), plane, 0,...  13.7 us
    all_to_all x1, blocking collectives, shards(): lax.all_to_all(fold(member, parts, members, NZ, jnp.bfloat16), 'z', 0, 0,...  12.7 us
    all_to_all x1, waiting for transfers between devices, shards(): parts = lax.all_to_all(grads, plane, 0, 0, tiled=True)  8.85 us
    pallas_call x5, Pallas kernels, absorb(): pl.pallas_call(functools.partial(piece_body, ranges, acc is not None, spl...  6.61 us
    all_to_all x1, starting transfers between devices, shards(): parts = lax.all_to_all(grads, plane, 0, 0, tiled=True)  6.28 us
    pallas_call x1, Pallas kernels, degrees(): pl.pallas_call(degree_body, in_specs=[SMEM, ANY], out_specs=VMEM, out_sha...  4.45 us
  transfers between devices with their start and end apart: 22, of which 8 were waited for; matrix products, arithmetic and copies ran while one was open for 2% of the time, Pallas kernels for 12%

profile of v2, /device:TPU:1, one launch (start us, length us, event | category | flops | bytes accessed | tf_op | source)
XLA Modules:
  0.0 114.0 jit_solution(11034082441050318025)
XLA Ops:
  0.6 3.3 %collective-permute-start.5 = (bf16[256,128,128]{2,1,0:T(8,128)(2,1)}, bf16[256,128,128]{2,1,0:T(8,128)(2,1)}, u32[]{:S(2)}, u32[]{:S(2)}) collective-permute-start(bf16[256,128,128]{2,1,0:T(8,128)(2,1)} %bitcast.89), channel_id=1, source_target_pairs={{0,2},{2,0},{4,6},{6,4},{8,10},{10,8},{12,14},{14,12},{16,18},{18,... | collective-permute-start | bytes 25165832 | tf_op jit(solution)/shard_map/ppermute | solution.py:40
  7.8 3.9 %collective-permute-start.3 = (bf16[512,128]{1,0:T(8,128)(2,1)S(1)}, bf16[512,128]{1,0:T(8,128)(2,1)S(1)}, u32[]{:S(2)}, u32[]{:S(2)}) collective-permute-start(bf16[512,128]{1,0:T(8,128)(2,1)S(1)} %constant_dynamic-update-slice_fusion.refs_0_), channel_id=1, source_target_pairs={{0,24},{2,226},{4,28},{6,230},{8,0},{10,234},{12,4},{14,238},{16,8... | collective-permute-start | bytes 393224 | tf_op jit(solution)/shard_map/ppermute | solution.py:40
  11.8 4.5 %shard_map.145.refs_5_ = f32[512,128]{1,0:T(8,128)S(1)} custom-call(s32[256]{0:T(256)S(1)} %broadcast_select_fusion.code_ref.refs_1_, bf16[256,128,128]{2,1,0:T(8,128)(2,1)} %bitcast.90), custom_call_target="tpu_custom_call" | custom-call | flops 8388608 | bytes 8388608 | tf_op jit(solution)/shard_map/pallas_call | solution.py:93
  16.2 2.4 %collective-permute-done.4.refs_3_ = bf16[512,128]{1,0:T(8,128)(2,1)S(1)} collective-permute-done((bf16[512,128]{1,0:T(8,128)(2,1)S(1)}, bf16[512,128]{1,0:T(8,128)(2,1)S(1)}, u32[]{:S(2)}, u32[]{:S(2)}) %collective-permute-start.4) | collective-permute-done | bytes 131104 | tf_op jit(solution)/shard_map/ppermute | solution.py:40
  21.5 2.6 %collective-permute-start.9 = (bf16[512,128]{1,0:T(8,128)(2,1)S(1)}, bf16[512,128]{1,0:T(8,128)(2,1)S(1)}, u32[]{:S(2)}, u32[]{:S(2)}) collective-permute-start(bf16[512,128]{1,0:T(8,128)(2,1)S(1)} %collective-permute-done.3.refs_2_), channel_id=1, source_target_pairs={{0,24},{2,226},{4,28},{6,230},{8,0},{10,234},{12,4},{14,238},{16,8... | collective-permute-start | bytes 393224 | tf_op jit(solution)/shard_map/ppermute | solution.py:40
  24.1 2.9 %collective-permute-start = (s32[256]{0:T(256)S(1)}, s32[256]{0:T(256)S(1)}, u32[]{:S(2)}, u32[]{:S(2)}) collective-permute-start(s32[256]{0:T(256)S(1)} %get-tuple-element.76), channel_id=1, source_target_pairs={{0,2},{2,0},{4,6},{6,4},{8,10},{10,8},{12,14},{14,12},{16,18},{18,... | collective-permute-start | bytes 3080 | tf_op jit(solution)/shard_map/ppermute | solution.py:40
  27.1 3.5 %shard_map.147.refs_5_.refs_8_.refs_6_ = bf16[2,64,2,128,128]{4,3,2,1,0:T(8,128)(2,1)S(1)} custom-call(s32[1]{0:T(128)} %bitcast.core_ref.refs_0_, bf16[64,2,2,128,128]{4,3,2,1,0:T(8,128)(2,1)} %bitcast.91, bf16[64,2,2,128,128]{4,3,2,1,0:T(8,128)(2,1)} %bitcast.70.mate_ref), custom_call_target="tpu_custom_call" | custom-call | bytes 16777216 | tf_op jit(solution)/shard_map/pallas_call | solution.py:123
  31.9 2.7 %collective-permute-start.11 = (bf16[2048,128]{1,0:T(8,128)(2,1)S(1)}, bf16[2048,128]{1,0:T(8,128)(2,1)S(1)}, u32[]{:S(2)}, u32[]{:S(2)}) collective-permute-start(bf16[2048,128]{1,0:T(8,128)(2,1)S(1)} %collective-permute-done.7.refs_5_), channel_id=1, source_target_pairs={{0,224},{2,26},{4,228},{6,30},{8,232},{10,2},{12,236},{14,6},{16,2... | collective-permute-start | bytes 1572872 | tf_op jit(solution)/shard_map/ppermute | solution.py:40
  34.6 2.7 %collective-permute-start.13 = (bf16[512,128]{1,0:T(8,128)(2,1)S(1)}, bf16[512,128]{1,0:T(8,128)(2,1)S(1)}, u32[]{:S(2)}, u32[]{:S(2)}) collective-permute-start(bf16[512,128]{1,0:T(8,128)(2,1)S(1)} %collective-permute-done.9.refs_0_), channel_id=1, source_target_pairs={{0,24},{2,226},{4,28},{6,230},{8,0},{10,234},{12,4},{14,238},{16,8... | collective-permute-start | bytes 393224 | tf_op jit(solution)/shard_map/ppermute | solution.py:40
  37.2 4.1 %collective-permute-done.12.refs_3_ = bf16[512,128]{1,0:T(8,128)(2,1)S(1)} collective-permute-done((bf16[512,128]{1,0:T(8,128)(2,1)S(1)}, bf16[512,128]{1,0:T(8,128)(2,1)S(1)}, u32[]{:S(2)}, u32[]{:S(2)}) %collective-permute-start.12) | collective-permute-done | bytes 131104 | tf_op jit(solution)/shard_map/ppermute | solution.py:40
  41.3 1.5 %collective-permute-done.10.fore.refs_6_ = bf16[2048,128]{1,0:T(8,128)(2,1)S(1)} collective-permute-done((bf16[2048,128]{1,0:T(8,128)(2,1)S(1)}, bf16[2048,128]{1,0:T(8,128)(2,1)S(1)}, u32[]{:S(2)}, u32[]{:S(2)}) %collective-permute-start.10) | collective-permute-done | bytes 524320 | tf_op jit(solution)/shard_map/ppermute | solution.py:40
  43.1 2.7 %collective-permute-start.17 = (bf16[2048,128]{1,0:T(8,128)(2,1)S(1)}, bf16[2048,128]{1,0:T(8,128)(2,1)S(1)}, u32[]{:S(2)}, u32[]{:S(2)}) collective-permute-start(bf16[2048,128]{1,0:T(8,128)(2,1)S(1)} %get-tuple-element.52.refs_7_), channel_id=1, source_target_pairs={{0,224},{2,26},{4,228},{6,30},{8,232},{10,2},{12,236},{14,6},{16,2... | collective-permute-start | bytes 1572872 | tf_op jit(solution)/shard_map/ppermute | solution.py:40
  46.8 2.1 %collective-permute-start.14 = (bf16[1024,128]{1,0:T(8,128)(2,1)S(1)}, bf16[1024,128]{1,0:T(8,128)(2,1)S(1)}, u32[]{:S(2)}, u32[]{:S(2)}) collective-permute-start(bf16[1024,128]{1,0:T(8,128)(2,1)S(1)} %slice.18), channel_id=1, source_target_pairs={{0,192},{2,18},{4,196},{6,22},{8,200},{10,26},{12,204},{14,30},{16... | collective-permute-start | bytes 786440 | tf_op jit(solution)/shard_map/ppermute | solution.py:40
  48.8 2.2 %shard_map.150 = (f32[1024,128]{1,0:T(8,128)S(1)}, f32[512,128]{1,0:T(8,128)S(1)}) custom-call(s32[1]{0:T(128)} %bitcast.core_ref.refs_0_, s32[256]{0:T(256)S(1)} %broadcast_select_fusion.code_ref.refs_1_, s32[256]{0:T(256)S(1)} %collective-permute-done.refs_2_, s32[64]{0:T(128)S(1)} %stack.259.refs_3_, ...), custom_call_target="tpu_custom_call", output_to_operand_aliasing={{1}: (10, {})} | custom-call | flops 536870912 | bytes 5242880 | tf_op jit(solution)/shard_map/pallas_call | solution.py:183
  51.0 3.0 %collective-permute-start.18 = (f32[256,128]{1,0:T(8,128)S(1)}, f32[256,128]{1,0:T(8,128)S(1)}, u32[]{:S(2)}, u32[]{:S(2)}) collective-permute-start(f32[256,128]{1,0:T(8,128)S(1)} %get-tuple-element.79), channel_id=1, source_target_pairs={{0,1},{1,0},{2,3},{3,2},{4,5},{5,4},{6,7},{7,6},{8,9},{9,8},{10,11... | collective-permute-start | bytes 393224 | tf_op jit(solution)/shard_map/ppermute | solution.py:277
  54.0 3.4 %collective-permute-done.17.refs_5_ = bf16[2048,128]{1,0:T(8,128)(2,1)S(1)} collective-permute-done((bf16[2048,128]{1,0:T(8,128)(2,1)S(1)}, bf16[2048,128]{1,0:T(8,128)(2,1)S(1)}, u32[]{:S(2)}, u32[]{:S(2)}) %collective-permute-start.17) | collective-permute-done | bytes 524320 | tf_op jit(solution)/shard_map/ppermute | solution.py:40
  60.9 3.2 %collective-permute-start.19 = (f32[512,128]{1,0:T(8,128)S(1)}, f32[512,128]{1,0:T(8,128)S(1)}, u32[]{:S(2)}, u32[]{:S(2)}) collective-permute-start(f32[512,128]{1,0:T(8,128)S(1)} %get-tuple-element.66), channel_id=1, source_target_pairs={{0,2},{2,0},{4,6},{6,4},{8,10},{10,8},{12,14},{14,12},{16,18},{18,... | collective-permute-start | bytes 786440 | tf_op jit(solution)/shard_map/ppermute | solution.py:40
  65.3 3.0 %collective-permute-start.20 = (bf16[256,128]{1,0:T(8,128)(2,1)S(1)}, bf16[256,128]{1,0:T(8,128)(2,1)S(1)}, u32[]{:S(2)}, u32[]{:S(2)}) collective-permute-start(bf16[256,128]{1,0:T(8,128)(2,1)S(1)} %fusion), channel_id=1, source_target_pairs={{0,1},{1,0},{2,3},{3,2},{4,5},{5,4},{6,7},{7,6},{8,9},{9,8},{10,11... | collective-permute-start | bytes 196616 | tf_op jit(solution)/shard_map/ppermute | solution.py:413
  68.5 1.5 %collective-permute-done.20.theirs = bf16[256,128]{1,0:T(8,128)(2,1)S(1)} collective-permute-done((bf16[256,128]{1,0:T(8,128)(2,1)S(1)}, bf16[256,128]{1,0:T(8,128)(2,1)S(1)}, u32[]{:S(2)}, u32[]{:S(2)}) %collective-permute-start.20) | collective-permute-done | bytes 65568 | tf_op jit(solution)/shard_map/ppermute | solution.py:413
  70.0 1.6 %shard_map.154 = (bf16[256,256]{1,0:T(8,128)(2,1)}, bf16[512,256]{1,0:T(8,128)(2,1)}) custom-call(bf16[256,128]{1,0:T(8,128)(2,1)S(1)} %copy-done, f32[256,128]{1,0:T(8,128)S(1)} %get-tuple-element.65.mine, f32[512,128]{1,0:T(8,128)S(1)} %collective-permute-done.19.mates, bf16[256,128]{1,0:T(8,128)(2,1)S(1)} %collective-permute-done.20.theirs, ...), custom_call_target="tpu_custom_call" | custom-call | flops 201326592 | bytes 2097152 | tf_op jit(solution)/shard_map/pallas_call | solution.py:334
  71.6 6.3 %all-to-all-start = ((bf16[32,16,256]{2,1,0:T(8,128)(2,1)}), bf16[32,16,256]{2,1,0:T(8,128)(2,1)S(1)}, u32[]{:S(2)}, u32[]{:S(2)}) async-start(bf16[32,16,256]{2,1,0:T(8,128)(2,1)} %bitcast.74), calls=%async_computation | async-start | bytes 524288 | tf_op jit(solution)/shard_map/all_to_all | solution.py:431
  77.9 8.8 %all-to-all-done = bf16[32,16,256]{2,1,0:T(8,128)(2,1)S(1)} async-done(((bf16[32,16,256]{2,1,0:T(8,128)(2,1)}), bf16[32,16,256]{2,1,0:T(8,128)(2,1)S(1)}, u32[]{:S(2)}, u32[]{:S(2)}) %all-to-all-start) | async-done | bytes 262176 | tf_op jit(solution)/shard_map/all_to_all | solution.py:431
  86.8 12.7 %all_to_all.33 = bf16[8,16,256]{2,1,0:T(8,128)(2,1)S(1)} all-to-all(bf16[8,16,256]{2,1,0:T(8,128)(2,1)S(1)} %bitcast.88), channel_id=1, replica_groups=mesh['z'=8,'x'=4,'yl'=2,'co'=2,'yh'=2] {'z'}, dimensions={0} | all-to-all | bytes 131072 | tf_op jit(solution)/shard_map/all_to_all | solution.py:432
  99.5 13.7 %all_to_all.34 = bf16[32,16,256]{2,1,0:T(8,128)(2,1)S(1)} all-to-all(bf16[32,16,256]{2,1,0:T(8,128)(2,1)S(1)} %bitcast.85), channel_id=1, replica_groups=mesh['z'=8,'x'=4,'yl'=2,'co'=2,'yh'=2] {'x','yl','co','yh'}, dimensions={0} | all-to-all | bytes 524288 | tf_op jit(solution)/shard_map/all_to_all | solution.py:433
  (61 shorter events, 14.9 us)
Async XLA Ops:
  0.6 18.0 %collective-permute-start.5 = (bf16[256,128,128]{2,1,0:T(8,128)(2,1)}, bf16[256,128,128]{2,1,0:T(8,128)(2,1)}, u32[]{:S(2)}, u32[]{:S(2)}) collective-permute-start(bf16[256,128,128]{2,1,0:T(8,128)(2,1)} %bitcast.89), channel_id=1, source_target_pairs={{0,2},{2,0},{4,6},{6,4},{8,10},{10,8},{12,14},{14,12},{16,18},{18,... | collective-permute-start | bytes 25165832 | tf_op jit(solution)/shard_map/ppermute | solution.py:40
  4.0 3.9 %collective-permute-start.1 = (bf16[256,128]{1,0:T(8,128)(2,1)}, bf16[256,128]{1,0:T(8,128)(2,1)S(1)}, u32[]{:S(2)}, u32[]{:S(2)}) collective-permute-start(bf16[256,128]{1,0:T(8,128)(2,1)} %feat.1), channel_id=1, source_target_pairs={{0,4},{2,6},{4,0},{6,2},{8,12},{10,14},{12,8},{14,10},{16,20},{18,... | collective-permute-start | bytes 196616 | tf_op jit(solution)/shard_map/ppermute | solution.py:40
  7.8 8.4 %collective-permute-start.3 = (bf16[512,128]{1,0:T(8,128)(2,1)S(1)}, bf16[512,128]{1,0:T(8,128)(2,1)S(1)}, u32[]{:S(2)}, u32[]{:S(2)}) collective-permute-start(bf16[512,128]{1,0:T(8,128)(2,1)S(1)} %constant_dynamic-update-slice_fusion.refs_0_), channel_id=1, source_target_pairs={{0,24},{2,226},{4,28},{6,230},{8,0},{10,234},{12,4},{14,238},{16,8... | collective-permute-start | bytes 393224 | tf_op jit(solution)/shard_map/ppermute | solution.py:40
  11.8 6.8 %collective-permute-start.4 = (bf16[512,128]{1,0:T(8,128)(2,1)S(1)}, bf16[512,128]{1,0:T(8,128)(2,1)S(1)}, u32[]{:S(2)}, u32[]{:S(2)}) collective-permute-start(bf16[512,128]{1,0:T(8,128)(2,1)S(1)} %constant_dynamic-update-slice_fusion.refs_0_), channel_id=1, source_target_pairs={{0,16},{2,66},{4,20},{6,70},{8,24},{10,74},{12,28},{14,78},{16,0},... | collective-permute-start | bytes 393224 | tf_op jit(solution)/shard_map/ppermute | solution.py:40
  11.8 6.8 %collective-permute-start.2 = (bf16[512,128]{1,0:T(8,128)(2,1)S(1)}, bf16[512,128]{1,0:T(8,128)(2,1)S(1)}, u32[]{:S(2)}, u32[]{:S(2)}) collective-permute-start(bf16[512,128]{1,0:T(8,128)(2,1)S(1)} %constant_dynamic-update-slice_fusion.refs_0_), channel_id=1, source_target_pairs={{0,8},{2,34},{4,12},{6,38},{8,16},{10,42},{12,20},{14,46},{16,24},... | collective-permute-start | bytes 393224 | tf_op jit(solution)/shard_map/ppermute | solution.py:40
  18.6 13.1 %collective-permute-start.6 = (bf16[2048,128]{1,0:T(8,128)(2,1)S(1)}, bf16[2048,128]{1,0:T(8,128)(2,1)S(1)}, u32[]{:S(2)}, u32[]{:S(2)}) collective-permute-start(bf16[2048,128]{1,0:T(8,128)(2,1)S(1)} %get-tuple-element.41.refs_4_), channel_id=1, source_target_pairs={{0,32},{2,10},{4,36},{6,14},{8,40},{10,18},{12,44},{14,22},{16,48}... | collective-permute-start | bytes 1572872 | tf_op jit(solution)/shard_map/ppermute | solution.py:40
  19.9 11.9 %collective-permute-start.7 = (bf16[2048,128]{1,0:T(8,128)(2,1)S(1)}, bf16[2048,128]{1,0:T(8,128)(2,1)S(1)}, u32[]{:S(2)}, u32[]{:S(2)}) collective-permute-start(bf16[2048,128]{1,0:T(8,128)(2,1)S(1)} %get-tuple-element.41.refs_4_), channel_id=1, source_target_pairs={{0,224},{2,26},{4,228},{6,30},{8,232},{10,2},{12,236},{14,6},{16,2... | collective-permute-start | bytes 1572872 | tf_op jit(solution)/shard_map/ppermute | solution.py:40
  21.4 10.4 %collective-permute-start.8 = (bf16[512,128]{1,0:T(8,128)(2,1)S(1)}, bf16[512,128]{1,0:T(8,128)(2,1)S(1)}, u32[]{:S(2)}, u32[]{:S(2)}) collective-permute-start(bf16[512,128]{1,0:T(8,128)(2,1)S(1)} %collective-permute-done.4.refs_3_), channel_id=1, source_target_pairs={{0,8},{2,34},{4,12},{6,38},{8,16},{10,42},{12,20},{14,46},{16,24},... | collective-permute-start | bytes 393224 | tf_op jit(solution)/shard_map/ppermute | solution.py:40
  21.5 10.3 %collective-permute-start.9 = (bf16[512,128]{1,0:T(8,128)(2,1)S(1)}, bf16[512,128]{1,0:T(8,128)(2,1)S(1)}, u32[]{:S(2)}, u32[]{:S(2)}) collective-permute-start(bf16[512,128]{1,0:T(8,128)(2,1)S(1)} %collective-permute-done.3.refs_2_), channel_id=1, source_target_pairs={{0,24},{2,226},{4,28},{6,230},{8,0},{10,234},{12,4},{14,238},{16,8... | collective-permute-start | bytes 393224 | tf_op jit(solution)/shard_map/ppermute | solution.py:40
  24.1 6.6 %collective-permute-start = (s32[256]{0:T(256)S(1)}, s32[256]{0:T(256)S(1)}, u32[]{:S(2)}, u32[]{:S(2)}) collective-permute-start(s32[256]{0:T(256)S(1)} %get-tuple-element.76), channel_id=1, source_target_pairs={{0,2},{2,0},{4,6},{6,4},{8,10},{10,8},{12,14},{14,12},{16,18},{18,... | collective-permute-start | bytes 3080 | tf_op jit(solution)/shard_map/ppermute | solution.py:40
  31.8 11.0 %collective-permute-start.10 = (bf16[2048,128]{1,0:T(8,128)(2,1)S(1)}, bf16[2048,128]{1,0:T(8,128)(2,1)S(1)}, u32[]{:S(2)}, u32[]{:S(2)}) collective-permute-start(bf16[2048,128]{1,0:T(8,128)(2,1)S(1)} %collective-permute-done.6.refs_4_), channel_id=1, source_target_pairs={{0,32},{2,10},{4,36},{6,14},{8,40},{10,18},{12,44},{14,22},{16,48}... | collective-permute-start | bytes 1572872 | tf_op jit(solution)/shard_map/ppermute | solution.py:40
  31.9 10.9 %collective-permute-start.11 = (bf16[2048,128]{1,0:T(8,128)(2,1)S(1)}, bf16[2048,128]{1,0:T(8,128)(2,1)S(1)}, u32[]{:S(2)}, u32[]{:S(2)}) collective-permute-start(bf16[2048,128]{1,0:T(8,128)(2,1)S(1)} %collective-permute-done.7.refs_5_), channel_id=1, source_target_pairs={{0,224},{2,26},{4,228},{6,30},{8,232},{10,2},{12,236},{14,6},{16,2... | collective-permute-start | bytes 1572872 | tf_op jit(solution)/shard_map/ppermute | solution.py:40
  34.6 6.8 %collective-permute-start.12 = (bf16[512,128]{1,0:T(8,128)(2,1)S(1)}, bf16[512,128]{1,0:T(8,128)(2,1)S(1)}, u32[]{:S(2)}, u32[]{:S(2)}) collective-permute-start(bf16[512,128]{1,0:T(8,128)(2,1)S(1)} %collective-permute-done.8.refs_1_), channel_id=1, source_target_pairs={{0,8},{2,34},{4,12},{6,38},{8,16},{10,42},{12,20},{14,46},{16,24},... | collective-permute-start | bytes 393224 | tf_op jit(solution)/shard_map/ppermute | solution.py:40
  34.6 6.8 %collective-permute-start.13 = (bf16[512,128]{1,0:T(8,128)(2,1)S(1)}, bf16[512,128]{1,0:T(8,128)(2,1)S(1)}, u32[]{:S(2)}, u32[]{:S(2)}) collective-permute-start(bf16[512,128]{1,0:T(8,128)(2,1)S(1)} %collective-permute-done.9.refs_0_), channel_id=1, source_target_pairs={{0,24},{2,226},{4,28},{6,230},{8,0},{10,234},{12,4},{14,238},{16,8... | collective-permute-start | bytes 393224 | tf_op jit(solution)/shard_map/ppermute | solution.py:40
  43.0 11.1 %collective-permute-start.16 = (bf16[2048,128]{1,0:T(8,128)(2,1)S(1)}, bf16[2048,128]{1,0:T(8,128)(2,1)S(1)}, u32[]{:S(2)}, u32[]{:S(2)}) collective-permute-start(bf16[2048,128]{1,0:T(8,128)(2,1)S(1)} %get-tuple-element.53), channel_id=1, source_target_pairs={{0,32},{2,10},{4,36},{6,14},{8,40},{10,18},{12,44},{14,22},{16,48}... | collective-permute-start | bytes 1572872 | tf_op jit(solution)/shard_map/ppermute | solution.py:40
  43.1 14.4 %collective-permute-start.17 = (bf16[2048,128]{1,0:T(8,128)(2,1)S(1)}, bf16[2048,128]{1,0:T(8,128)(2,1)S(1)}, u32[]{:S(2)}, u32[]{:S(2)}) collective-permute-start(bf16[2048,128]{1,0:T(8,128)(2,1)S(1)} %get-tuple-element.52.refs_7_), channel_id=1, source_target_pairs={{0,224},{2,26},{4,228},{6,30},{8,232},{10,2},{12,236},{14,6},{16,2... | collective-permute-start | bytes 1572872 | tf_op jit(solution)/shard_map/ppermute | solution.py:40
  45.8 13.2 %collective-permute-start.15 = (bf16[1024,128]{1,0:T(8,128)(2,1)S(1)}, bf16[1024,128]{1,0:T(8,128)(2,1)S(1)}, u32[]{:S(2)}, u32[]{:S(2)}) collective-permute-start(bf16[1024,128]{1,0:T(8,128)(2,1)S(1)} %slice.19), channel_id=1, source_target_pairs={{0,64},{2,18},{4,68},{6,22},{8,72},{10,26},{12,76},{14,30},{16,80}... | collective-permute-start | bytes 786440 | tf_op jit(solution)/shard_map/ppermute | solution.py:40
  46.8 13.2 %collective-permute-start.14 = (bf16[1024,128]{1,0:T(8,128)(2,1)S(1)}, bf16[1024,128]{1,0:T(8,128)(2,1)S(1)}, u32[]{:S(2)}, u32[]{:S(2)}) collective-permute-start(bf16[1024,128]{1,0:T(8,128)(2,1)S(1)} %slice.18), channel_id=1, source_target_pairs={{0,192},{2,18},{4,196},{6,22},{8,200},{10,26},{12,204},{14,30},{16... | collective-permute-start | bytes 786440 | tf_op jit(solution)/shard_map/ppermute | solution.py:40
  51.0 8.0 %collective-permute-start.18 = (f32[256,128]{1,0:T(8,128)S(1)}, f32[256,128]{1,0:T(8,128)S(1)}, u32[]{:S(2)}, u32[]{:S(2)}) collective-permute-start(f32[256,128]{1,0:T(8,128)S(1)} %get-tuple-element.79), channel_id=1, source_target_pairs={{0,1},{1,0},{2,3},{3,2},{4,5},{5,4},{6,7},{7,6},{8,9},{9,8},{10,11... | collective-permute-start | bytes 393224 | tf_op jit(solution)/shard_map/ppermute | solution.py:277
  59.0 11.0 %copy-start = (bf16[256,128]{1,0:T(8,128)(2,1)S(1)}, bf16[256,128]{1,0:T(8,128)(2,1)}, u32[]{:S(2)}) copy-start(bf16[256,128]{1,0:T(8,128)(2,1)} %feat.1) | copy-start | bytes 196612
  59.0 11.0 %copy-start.1 = (bf16[128,256]{1,0:T(8,128)(2,1)S(1)}, bf16[128,256]{1,0:T(8,128)(2,1)}, u32[]{:S(2)}) copy-start(bf16[128,256]{1,0:T(8,128)(2,1)} %w_self.1) | copy-start | bytes 196612
  60.9 4.3 %collective-permute-start.19 = (f32[512,128]{1,0:T(8,128)S(1)}, f32[512,128]{1,0:T(8,128)S(1)}, u32[]{:S(2)}, u32[]{:S(2)}) collective-permute-start(f32[512,128]{1,0:T(8,128)S(1)} %get-tuple-element.66), channel_id=1, source_target_pairs={{0,2},{2,0},{4,6},{6,4},{8,10},{10,8},{12,14},{14,12},{16,18},{18,... | collective-permute-start | bytes 786440 | tf_op jit(solution)/shard_map/ppermute | solution.py:40
  65.3 4.7 %collective-permute-start.20 = (bf16[256,128]{1,0:T(8,128)(2,1)S(1)}, bf16[256,128]{1,0:T(8,128)(2,1)S(1)}, u32[]{:S(2)}, u32[]{:S(2)}) collective-permute-start(bf16[256,128]{1,0:T(8,128)(2,1)S(1)} %fusion), channel_id=1, source_target_pairs={{0,1},{1,0},{2,3},{3,2},{4,5},{5,4},{6,7},{7,6},{8,9},{9,8},{10,11... | collective-permute-start | bytes 196616 | tf_op jit(solution)/shard_map/ppermute | solution.py:413
  71.6 15.2 %all-to-all-start = ((bf16[32,16,256]{2,1,0:T(8,128)(2,1)}), bf16[32,16,256]{2,1,0:T(8,128)(2,1)S(1)}, u32[]{:S(2)}, u32[]{:S(2)}) async-start(bf16[32,16,256]{2,1,0:T(8,128)(2,1)} %bitcast.74), calls=%async_computation | async-start | bytes 524288 | tf_op jit(solution)/shard_map/all_to_all | solution.py:431
  (4 other events, 39.3 us)
